TPU v7x, 32 devices: a whole 2x2x4 slice. The times are simulated.
32 devices in a mesh: section: 2 (over core), fsdp: 4 (over z), rep: 4 (over y, x).
Axes of the slice: x: 2, y: 2, z: 4, core: 2. Of those that a mesh axis runs over, the one named last changes fastest.
Arguments:
- tokens: bfloat16 [2, 4, 512, 768], P('section', 'rep', 'fsdp'), may hold values from -6 to 6
- lengths: int32 [2, 4], P(None, 'rep'), may hold values from 256 to 512, as said below
- cotangent: bfloat16 [2, 4, 512, 768], P('section', 'rep', 'fsdp'), may hold values from -6 to 6
- w_qkv: bfloat16 [2, 768, 2304], P('section', 'fsdp'), may hold values from -0.21875 to 0.21875
- w_out: bfloat16 [2, 768, 768], P('section', 'fsdp'), may hold values from -0.875 to 0.875
- norm1_gain: bfloat16 [2, 768], P('section', 'fsdp'), may hold values from 0.5 to 1.5
- norm1_bias: bfloat16 [2, 768], P('section', 'fsdp'), may hold values from -1.75 to 1.75
- w_gate: bfloat16 [2, 768, 3072], P('section', 'fsdp'), may hold values from -0.21875 to 0.21875
- w_up: bfloat16 [2, 768, 3072], P('section', 'fsdp'), may hold values from -0.21875 to 0.21875
- w_down: bfloat16 [2, 3072, 768], P('section', 'fsdp'), may hold values from -0.109375 to 0.109375
- norm2_gain: bfloat16 [2, 768], P('section', 'fsdp'), may hold values from 0.5 to 1.5
- norm2_bias: bfloat16 [2, 768], P('section', 'fsdp'), may hold values from -1.75 to 1.75
Outputs:
- output: bfloat16 [2, 4, 512, 768], P('section', 'rep', 'fsdp')
- token_grad: bfloat16 [2, 4, 512, 768], P('section', 'rep', 'fsdp')
- grad_w_qkv: float32 [2, 768, 2304], P('section', 'fsdp')
- grad_w_out: float32 [2, 768, 768], P('section', 'fsdp')
- grad_norm1_gain: float32 [2, 768], P('section', 'fsdp')
- grad_norm1_bias: float32 [2, 768], P('section', 'fsdp')
- grad_w_gate: float32 [2, 768, 3072], P('section', 'fsdp')
- grad_w_up: float32 [2, 768, 3072], P('section', 'fsdp')
- grad_w_down: float32 [2, 3072, 768], P('section', 'fsdp')
- grad_norm2_gain: float32 [2, 768], P('section', 'fsdp')
- grad_norm2_bias: float32 [2, 768], P('section', 'fsdp')
Inputs may be any that keep to these rules, and one draw needn't show every extreme that they name: `lengths`: in every group one of the 2 sequences fills all 512 slots; the others fill half of them or more.
All inputs are finite; a program needn't handle non-finite values.
Results may differ from a plain program's by a relative error of at most 0.02.
Values may be sent and summed in bfloat16 or wider, within the bound.
A program may use at most 320 MiB of HBM per device.

v0:
```python
import jax
import jax.numpy as jnp
from jax import lax
from jax.sharding import PartitionSpec as P

HEADS = 12
HEAD_DIM = 64


norm_eps = 1e-05
masked_score = -1000000000.0


def partner(block, axis, distance):
    count = lax.axis_size(axis)
    route = []
    for low in range(count):
        high = low | 1 << distance
        if high != low and high < count:
            route += [(low, high), (high, low)]
    return lax.ppermute(block, axis, route)


def shifted(value, axis, steps):
    count = lax.axis_size(axis)
    initial, last = (max(0, -steps), min(count, count - steps))
    return lax.ppermute(value, axis, [(source, source + steps) for source in range(initial, last)])


def norm_rows(values, norm_gain, offset):
    centre = values - jnp.mean(values, axis=-1, keepdims=True)
    inverse = lax.rsqrt(jnp.mean(centre * centre, axis=-1, keepdims=True) + norm_eps)
    normed = centre * inverse
    return (normed * norm_gain + offset, normed, inverse)


def norm_back(grad_out, normed, inverse, norm_gain):
    scaled = grad_out * norm_gain
    return inverse * (
        scaled
        - jnp.mean(scaled, axis=-1, keepdims=True)
        - normed * jnp.mean(scaled * normed, axis=-1, keepdims=True)
    )


def rotary_tables(first_slot, row_count):
    half_dim = HEAD_DIM // 2
    inverse_freq = 1000.0 ** (-2.0 * jnp.arange(half_dim, dtype=jnp.float32) / HEAD_DIM)
    places = (first_slot + jnp.arange(row_count)).astype(jnp.float32)
    angles = places[:, None] * inverse_freq[None, :]
    angles = jnp.concatenate([angles, angles], axis=-1)[:, None, :]
    return (jnp.cos(angles), jnp.sin(angles))


def turn_half(values):
    half_dim = values.shape[-1] // 2
    return jnp.concatenate([-values[..., half_dim:], values[..., :half_dim]], axis=-1)


def rotate(values, cosine_table, sine_table):
    return values * cosine_table + turn_half(values) * sine_table


def rotate_back(values, cosine_table, sine_table):
    return values * cosine_table - turn_half(values) * sine_table


def masked_scores(query_rot, key_all, live_keys):
    key_heads = key_all.reshape(key_all.shape[0], HEADS, HEAD_DIM)
    scores = jnp.einsum(
        "qhd,khd->hqk", query_rot, key_heads, preferred_element_type=jnp.float32
    ) * HEAD_DIM ** (-0.5)
    return jnp.where(live_keys[None, None, :], scores, masked_score)


def batch_length(length_column, batch_now):
    picked = jnp.clip(batch_now, 0, length_column.shape[0] - 1)
    return lax.dynamic_index_in_dim(length_column, picked, 0, keepdims=False)


def layer_forward(inputs, weights, live_keys, cosine_table, sine_table):
    w_qkv, w_out, gain_one, offset_one, w_gate, w_up, w_down, gain_two, offset_two = weights
    row_count, model_width = inputs.shape
    head_shape = (row_count, HEADS, HEAD_DIM)
    inputs_low = inputs.astype(jnp.bfloat16)
    joined = jnp.dot(inputs_low, w_qkv, preferred_element_type=jnp.float32)
    query_rot = rotate(
        joined[:, :model_width].reshape(head_shape), cosine_table, sine_table
    ).astype(jnp.bfloat16)
    key_own = (
        rotate(
            joined[:, model_width : 2 * model_width].reshape(head_shape), cosine_table, sine_table
        )
        .reshape(row_count, model_width)
        .astype(jnp.bfloat16)
    )
    value_own = joined[:, 2 * model_width :].astype(jnp.bfloat16)
    key_all, value_all = (
        lax.all_gather(key_own, "fsdp", axis=0, tiled=True),
        lax.all_gather(value_own, "fsdp", axis=0, tiled=True),
    )
    scores = masked_scores(query_rot, key_all, live_keys)
    highest = jnp.max(scores, axis=-1, keepdims=True)
    log_total = highest + jnp.log(jnp.sum(jnp.exp(scores - highest), axis=-1, keepdims=True))
    softmax_weights = jnp.exp(scores - log_total).astype(jnp.bfloat16)
    value_heads = value_all.reshape(value_all.shape[0], HEADS, HEAD_DIM)
    mixed_heads = jnp.einsum(
        "hqk,khd->qhd", softmax_weights, value_heads, preferred_element_type=jnp.float32
    )
    mixed_heads = mixed_heads.reshape(row_count, model_width).astype(jnp.bfloat16)
    attended = jnp.dot(mixed_heads, w_out, preferred_element_type=jnp.float32)
    hidden, normed_one, inverse_one = norm_rows(inputs + attended, gain_one, offset_one)
    hidden_low = hidden.astype(jnp.bfloat16)
    gate_proj = jnp.dot(hidden_low, w_gate, preferred_element_type=jnp.float32)
    upward = jnp.dot(hidden_low, w_up, preferred_element_type=jnp.float32)
    product = (jax.nn.silu(gate_proj) * upward).astype(jnp.bfloat16)
    mlp_out = jnp.dot(product, w_down, preferred_element_type=jnp.float32)
    result, normed_two, inverse_two = norm_rows(hidden + mlp_out, gain_two, offset_two)
    key_saved, value_saved = (key_all, value_all)
    kept_state = (
        inputs_low,
        query_rot,
        key_saved,
        value_saved,
        log_total,
        mixed_heads,
        normed_one,
        inverse_one,
        hidden_low,
        gate_proj,
        upward,
        product,
        normed_two,
        inverse_two,
    )
    return (result, kept_state)


def layer_backward(grad_out, kept_state, weights, live_keys, cosine_table, sine_table):
    w_qkv, w_out, gain_one, offset_one, w_gate, w_up, w_down, gain_two, offset_two = weights
    (
        inputs_low,
        query_rot,
        key_saved,
        value_saved,
        log_total,
        mixed_heads,
        normed_one,
        inverse_one,
        hidden_low,
        gate_proj,
        upward,
        product,
        normed_two,
        inverse_two,
    ) = kept_state
    row_count, model_width = inputs_low.shape
    head_shape = (row_count, HEADS, HEAD_DIM)
    key_all, value_all = (key_saved, value_saved)
    grad_gain_two = jnp.sum(grad_out * normed_two, axis=0)
    grad_offset_two = jnp.sum(grad_out, axis=0)
    grad_second = norm_back(grad_out, normed_two, inverse_two, gain_two)
    grad_fed = grad_second.astype(jnp.bfloat16)
    grad_product = jnp.einsum("rd,fd->rf", grad_fed, w_down, preferred_element_type=jnp.float32)
    grad_w_down = jnp.einsum("rf,rd->fd", product, grad_fed, preferred_element_type=jnp.float32)
    sigmoid_gate = jax.nn.sigmoid(gate_proj)
    silu_gate = gate_proj * sigmoid_gate
    grad_gate = (
        grad_product * upward * sigmoid_gate * (1.0 + gate_proj * (1.0 - sigmoid_gate))
    ).astype(jnp.bfloat16)
    grad_upward = (grad_product * silu_gate).astype(jnp.bfloat16)
    grad_hidden = grad_second + jnp.einsum(
        "rf,df->rd", grad_gate, w_gate, preferred_element_type=jnp.float32
    )
    grad_hidden = grad_hidden + jnp.einsum(
        "rf,df->rd", grad_upward, w_up, preferred_element_type=jnp.float32
    )
    grad_w_gate = jnp.einsum("rd,rf->df", hidden_low, grad_gate, preferred_element_type=jnp.float32)
    grad_w_up = jnp.einsum("rd,rf->df", hidden_low, grad_upward, preferred_element_type=jnp.float32)
    grad_gain_one = jnp.sum(grad_hidden * normed_one, axis=0)
    grad_offset_one = jnp.sum(grad_hidden, axis=0)
    grad_first = norm_back(grad_hidden, normed_one, inverse_one, gain_one)
    grad_attended = grad_first.astype(jnp.bfloat16)
    grad_w_out = jnp.einsum(
        "rd,re->de", mixed_heads, grad_attended, preferred_element_type=jnp.float32
    )
    grad_mixed = (
        jnp.einsum("re,de->rd", grad_attended, w_out, preferred_element_type=jnp.float32)
        .astype(jnp.bfloat16)
        .reshape(head_shape)
    )
    scores = masked_scores(query_rot, key_all, live_keys)
    attention = jnp.exp(scores - log_total)
    key_count = key_all.shape[0]
    key_heads = key_all.reshape(key_count, HEADS, HEAD_DIM)
    value_heads = value_all.reshape(key_count, HEADS, HEAD_DIM)
    grad_attention = jnp.einsum(
        "qhd,khd->hqk", grad_mixed, value_heads, preferred_element_type=jnp.float32
    )
    centre_term = jnp.sum(grad_attention * attention, axis=-1, keepdims=True)
    grad_scores = (attention * (grad_attention - centre_term)).astype(jnp.bfloat16)
    score_scale = HEAD_DIM ** (-0.5)
    grad_query = (
        jnp.einsum("hqk,khd->qhd", grad_scores, key_heads, preferred_element_type=jnp.float32)
        * score_scale
    )
    attention_low = attention.astype(jnp.bfloat16)
    grad_value_all = jnp.einsum(
        "hqk,qhd->khd", attention_low, grad_mixed, preferred_element_type=jnp.float32
    )
    grad_key_all = (
        jnp.einsum("hqk,qhd->khd", grad_scores, query_rot, preferred_element_type=jnp.float32)
        * score_scale
    )
    grad_key, grad_value = (
        lax.psum_scatter(
            grad_key_all.reshape(key_count, model_width).astype(jnp.bfloat16),
            "fsdp",
            scatter_dimension=0,
            tiled=True,
        ).astype(jnp.float32),
        lax.psum_scatter(
            grad_value_all.reshape(key_count, model_width).astype(jnp.bfloat16),
            "fsdp",
            scatter_dimension=0,
            tiled=True,
        ).astype(jnp.float32),
    )
    grad_joined = jnp.concatenate(
        [
            rotate_back(grad_query, cosine_table, sine_table).reshape(row_count, model_width),
            rotate_back(grad_key.reshape(head_shape), cosine_table, sine_table).reshape(
                row_count, model_width
            ),
            grad_value,
        ],
        axis=1,
    ).astype(jnp.bfloat16)
    grad_w_qkv = jnp.einsum(
        "rd,re->de", inputs_low, grad_joined, preferred_element_type=jnp.float32
    )
    grad_inputs = grad_first + jnp.einsum(
        "re,de->rd", grad_joined, w_qkv, preferred_element_type=jnp.float32
    )
    weight_grads = (
        grad_w_qkv,
        grad_w_out,
        grad_gain_one,
        grad_offset_one,
        grad_w_gate,
        grad_w_up,
        grad_w_down,
        grad_gain_two,
        grad_offset_two,
    )
    return (grad_inputs, weight_grads)


def shards(
    tokens,
    lengths,
    cotangent,
    w_qkv,
    w_out,
    norm1_gain,
    norm1_bias,
    w_gate,
    w_up,
    w_down,
    norm2_gain,
    norm2_bias,
):
    section_index = lax.axis_index("section")
    fsdp_index = lax.axis_index("fsdp")
    is_first = section_index == 0
    row_count = tokens.shape[2]
    model_width = tokens.shape[3]
    slot_count = row_count * lax.axis_size("fsdp")
    micro_count = lengths.shape[0]
    weights = (
        lax.all_gather(w_qkv[0], "fsdp", axis=0, tiled=True),
        lax.all_gather(w_out[0], "fsdp", axis=0, tiled=True),
        lax.all_gather(norm1_gain[0], "fsdp", axis=0, tiled=True),
        lax.all_gather(norm1_bias[0], "fsdp", axis=0, tiled=True),
        lax.all_gather(w_gate[0], "fsdp", axis=0, tiled=True),
        lax.all_gather(w_up[0], "fsdp", axis=0, tiled=True),
        lax.all_gather(w_down[0], "fsdp", axis=0, tiled=True),
        lax.all_gather(norm2_gain[0], "fsdp", axis=0, tiled=True),
        lax.all_gather(norm2_bias[0], "fsdp", axis=0, tiled=True),
    )
    own_tokens = tokens[0, 0]
    own_cotangent = cotangent[0, 0]
    arrived = partner(jnp.where(is_first, own_cotangent, own_tokens), "section", 0)
    batch_tokens = [
        jnp.where(is_first, own_tokens, arrived),
        jnp.where(is_first, arrived, own_tokens),
    ]
    batch_cotangents = [
        jnp.where(is_first, own_cotangent, arrived),
        jnp.where(is_first, arrived, own_cotangent),
    ]
    cosine_table, sine_table = rotary_tables(fsdp_index * row_count, row_count)
    row_slots = fsdp_index * row_count + jnp.arange(row_count)
    key_slots = jnp.arange(slot_count)
    length_column = lengths[:, 0]
    empty_rows = jnp.zeros((row_count, model_width), jnp.bfloat16)
    carried = empty_rows
    kept_list = []
    layer_outputs = []
    for tick_index in range(micro_count + 1):
        length_now = batch_length(length_column, tick_index - section_index)
        fresh_rows = batch_tokens[tick_index] if tick_index < micro_count else empty_rows
        inputs = jnp.where(is_first, fresh_rows, carried).astype(jnp.float32)
        result, kept_state = layer_forward(
            inputs, weights, key_slots < length_now, cosine_table, sine_table
        )
        result_low = result.astype(jnp.bfloat16)
        kept_list.append(kept_state)
        layer_outputs.append(result_low)
        if tick_index < micro_count:
            carried = shifted(result_low, "section", 1)
    arriving = empty_rows
    totals = None
    owned_total = None
    input_grads = []
    for tick_index in range(micro_count + 1):
        batch_now = tick_index - 1 + section_index
        length_now = batch_length(length_column, batch_now)
        is_valid = (batch_now >= 0) & (batch_now < micro_count)
        seed_rows = batch_cotangents[tick_index] if tick_index < micro_count else empty_rows
        seed_grad = (
            seed_rows.astype(jnp.float32) * (row_slots < length_now).astype(jnp.float32)[:, None]
        )
        grad_out = jnp.where(
            is_valid, jnp.where(is_first, arriving.astype(jnp.float32), seed_grad), 0.0
        )
        earlier_state = kept_list[max(tick_index - 1, 0)]
        later_state = kept_list[min(tick_index + 1, micro_count)]
        kept_state = jax.tree.map(
            lambda first_arr, second_arr: jnp.where(is_first, first_arr, second_arr),
            earlier_state,
            later_state,
        )
        grad_inputs, weight_grads = layer_backward(
            grad_out, kept_state, weights, key_slots < length_now, cosine_table, sine_table
        )
        grad_low = grad_inputs.astype(jnp.bfloat16)
        input_grads.append(grad_low)
        if tick_index < micro_count:
            arriving = shifted(grad_low, "section", -1)
        totals = weight_grads if totals is None else jax.tree.map(jnp.add, totals, weight_grads)
    shares = (
        lax.psum_scatter(
            totals[0].astype(jnp.bfloat16), "fsdp", scatter_dimension=0, tiled=True
        ).astype(jnp.float32),
        lax.psum_scatter(
            totals[1].astype(jnp.bfloat16), "fsdp", scatter_dimension=0, tiled=True
        ).astype(jnp.float32),
        lax.psum_scatter(
            totals[2].astype(jnp.bfloat16), "fsdp", scatter_dimension=0, tiled=True
        ).astype(jnp.float32),
        lax.psum_scatter(
            totals[3].astype(jnp.bfloat16), "fsdp", scatter_dimension=0, tiled=True
        ).astype(jnp.float32),
        lax.psum_scatter(
            totals[4].astype(jnp.bfloat16), "fsdp", scatter_dimension=0, tiled=True
        ).astype(jnp.float32),
        lax.psum_scatter(
            totals[5].astype(jnp.bfloat16), "fsdp", scatter_dimension=0, tiled=True
        ).astype(jnp.float32),
        lax.psum_scatter(
            totals[6].astype(jnp.bfloat16), "fsdp", scatter_dimension=0, tiled=True
        ).astype(jnp.float32),
        lax.psum_scatter(
            totals[7].astype(jnp.bfloat16), "fsdp", scatter_dimension=0, tiled=True
        ).astype(jnp.float32),
        lax.psum_scatter(
            totals[8].astype(jnp.bfloat16), "fsdp", scatter_dimension=0, tiled=True
        ).astype(jnp.float32),
    )
    owned_total = (
        lax.psum(shares[0].astype(jnp.bfloat16), "rep").astype(jnp.float32),
        lax.psum(shares[1].astype(jnp.bfloat16), "rep").astype(jnp.float32),
        lax.psum(shares[2].astype(jnp.bfloat16), "rep").astype(jnp.float32),
        lax.psum(shares[3].astype(jnp.bfloat16), "rep").astype(jnp.float32),
        lax.psum(shares[4].astype(jnp.bfloat16), "rep").astype(jnp.float32),
        lax.psum(shares[5].astype(jnp.bfloat16), "rep").astype(jnp.float32),
        lax.psum(shares[6].astype(jnp.bfloat16), "rep").astype(jnp.float32),
        lax.psum(shares[7].astype(jnp.bfloat16), "rep").astype(jnp.float32),
        lax.psum(shares[8].astype(jnp.bfloat16), "rep").astype(jnp.float32),
    )
    outgoing = jnp.where(is_first, input_grads[2], layer_outputs[1])
    returned = partner(outgoing, "section", 0)
    output_rows = jnp.where(is_first, returned, layer_outputs[2])
    grad_rows = jnp.where(is_first, input_grads[1], returned)
    return (
        output_rows[None, None],
        grad_rows[None, None],
        owned_total[0][None],
        owned_total[1][None],
        owned_total[2][None],
        owned_total[3][None],
        owned_total[4][None],
        owned_total[5][None],
        owned_total[6][None],
        owned_total[7][None],
        owned_total[8][None],
    )


def solution(mesh):
    return jax.shard_map(
        shards,
        mesh=mesh,
        in_specs=(
            P("section", "rep", "fsdp", None),
            P(None, "rep"),
            P("section", "rep", "fsdp", None),
            P("section", "fsdp", None),
            P("section", "fsdp", None),
            P("section", "fsdp"),
            P("section", "fsdp"),
            P("section", "fsdp", None),
            P("section", "fsdp", None),
            P("section", "fsdp", None),
            P("section", "fsdp"),
            P("section", "fsdp"),
        ),
        out_specs=(
            P("section", "rep", "fsdp", None),
            P("section", "rep", "fsdp", None),
            P("section", "fsdp", None),
            P("section", "fsdp", None),
            P("section", "fsdp"),
            P("section", "fsdp"),
            P("section", "fsdp", None),
            P("section", "fsdp", None),
            P("section", "fsdp", None),
            P("section", "fsdp"),
            P("section", "fsdp"),
        ),
        check_vma=False,
    )
```

profile of v0, /device:TPU:0, one launch (start us, length us, event | category | flops | bytes accessed | tf_op | source)
XLA Modules:
  0.0 1232.8 jit_solution(8866171826760589691)
XLA Ops:
  13.5 13.3 %all-reduce.11 = (bf16[768]{0:T(1024)(128)(2,1)S(1)}, bf16[768]{0:T(1024)(128)(2,1)S(1)}, bf16[768]{0:T(1024)(128)(2,1)S(1)}, bf16[768]{0:T(1024)(128)(2,1)S(1)}) all-reduce(bf16[768]{0:T(1024)(128)(2,1)S(1)} %dynamic-update-slice.1, bf16[768]{0:T(1024)(128)(2,1)S(1)} %dynamic-update-slice, ...), channel_id=5, replica_groups=mesh['section'=2,'fsdp'=4,'rep'=4] {'fsdp'}, use_global_device_ids=true, to_apply=%add.1 | all-reduce | flops 3072 | bytes 12288
  30.4 52.1 %all-gather.15.cloned.1.call-done = bf16[1,768,2304]{2,1,0:T(8,128)(2,1)} async-done(((bf16[1,192,2304]{2,1,0:T(8,128)(2,1)}), bf16[1,768,2304]{2,1,0:T(8,128)(2,1)}) %all-gather.15.cloned.1.call-update) | async-done | bytes 3538960 | tf_op jit(solution)/shard_map/all_gather | solution.py:281
  86.3 26.7 %all_gather.46 = bf16[512,768]{1,0:T(8,128)(2,1)S(1)} all-gather(bf16[128,768]{1,0:T(8,128)(2,1)S(1)} %slice.188), channel_id=1, replica_groups=mesh['section'=2,'fsdp'=4,'rep'=4] {'fsdp'}, dimensions={0}, use_global_device_ids=true | all-gather | bytes 983040 | tf_op jit(solution)/shard_map/all_gather | solution.py:100
  116.0 20.0 %all_gather.47 = bf16[512,768]{1,0:T(8,128)(2,1)S(1)} all-gather(bf16[128,768]{1,0:T(8,128)(2,1)S(1)} %get-tuple-element.80), channel_id=1, replica_groups=mesh['section'=2,'fsdp'=4,'rep'=4] {'fsdp'}, dimensions={0}, use_global_device_ids=true | all-gather | bytes 983040 | tf_op jit(solution)/shard_map/all_gather | solution.py:99
  141.1 75.0 %all-gather.19.cloned.1.call-done = bf16[1,768,3072]{2,1,0:T(8,128)(2,1)} async-done(((bf16[1,192,3072]{2,1,0:T(8,128)(2,1)}), bf16[1,768,3072]{2,1,0:T(8,128)(2,1)}) %all-gather.19.cloned.1.call-update) | async-done | bytes 4718608 | tf_op jit(solution)/shard_map/all_gather | solution.py:285
  220.4 85.0 %all-gather.21.cloned.1.call-done = bf16[1,768,3072]{2,1,0:T(8,128)(2,1)} async-done(((bf16[1,192,3072]{2,1,0:T(8,128)(2,1)}), bf16[1,768,3072]{2,1,0:T(8,128)(2,1)}) %all-gather.21.cloned.1.call-update) | async-done | bytes 4718608 | tf_op jit(solution)/shard_map/all_gather | solution.py:286
  310.5 84.3 %all-gather.23.cloned.1.call-done = bf16[1,3072,768]{2,1,0:T(8,128)(2,1)} async-done(((bf16[1,768,768]{2,1,0:T(8,128)(2,1)}), bf16[1,3072,768]{2,1,0:T(8,128)(2,1)}) %all-gather.23.cloned.1.call-update) | async-done | bytes 4718608 | tf_op jit(solution)/shard_map/all_gather | solution.py:287
  405.2 17.8 %all_gather.56 = bf16[512,768]{1,0:T(8,128)(2,1)S(1)} all-gather(bf16[128,768]{1,0:T(8,128)(2,1)S(1)} %slice.187), channel_id=1, replica_groups=mesh['section'=2,'fsdp'=4,'rep'=4] {'fsdp'}, dimensions={0}, use_global_device_ids=true | all-gather | bytes 983040 | tf_op jit(solution)/shard_map/all_gather | solution.py:100
  426.0 17.6 %all_gather.57 = bf16[512,768]{1,0:T(8,128)(2,1)S(1)} all-gather(bf16[128,768]{1,0:T(8,128)(2,1)S(1)} %get-tuple-element.78), channel_id=1, replica_groups=mesh['section'=2,'fsdp'=4,'rep'=4] {'fsdp'}, dimensions={0}, use_global_device_ids=true | all-gather | bytes 983040 | tf_op jit(solution)/shard_map/all_gather | solution.py:99
  469.6 18.6 %all_gather.58 = bf16[512,768]{1,0:T(8,128)(2,1)} all-gather(bf16[128,768]{1,0:T(8,128)(2,1)S(1)} %slice.186), channel_id=1, replica_groups=mesh['section'=2,'fsdp'=4,'rep'=4] {'fsdp'}, dimensions={0}, use_global_device_ids=true | all-gather | bytes 983040 | tf_op jit(solution)/shard_map/all_gather | solution.py:100
  491.7 15.8 %all_gather.59 = bf16[512,768]{1,0:T(8,128)(2,1)S(1)} all-gather(bf16[128,768]{1,0:T(8,128)(2,1)S(1)} %get-tuple-element.76), channel_id=1, replica_groups=mesh['section'=2,'fsdp'=4,'rep'=4] {'fsdp'}, dimensions={0}, use_global_device_ids=true | all-gather | bytes 983040 | tf_op jit(solution)/shard_map/all_gather | solution.py:99
  562.3 14.7 %reduce-scatter.36.cloned.1.call-done = bf16[128,768]{1,0:T(8,128)(2,1)} async-done(((bf16[512,768]{1,0:T(8,128)(2,1)}), bf16[128,768]{1,0:T(8,128)(2,1)}) %reduce-scatter.36.cloned.1.call-update) | async-done | bytes 196624
  625.1 8.2 reduce-scatter.38.cloned.1.call-done
  638.8 19.4 %reduce-scatter.40.cloned.1.call-done = bf16[128,768]{1,0:T(8,128)(2,1)} async-done(((bf16[512,768]{1,0:T(8,128)(2,1)}), bf16[128,768]{1,0:T(8,128)(2,1)}) %reduce-scatter.40.cloned.1.call-update) | async-done | bytes 196624
  703.3 5.3 fusion.196
  714.7 20.9 %reduce-scatter.44.cloned.1.call-done = bf16[128,768]{1,0:T(8,128)(2,1)} async-done(((bf16[512,768]{1,0:T(8,128)(2,1)}), bf16[128,768]{1,0:T(8,128)(2,1)}) %reduce-scatter.44.cloned.1.call-update) | async-done | bytes 196624
  736.7 8.0 add_convert_fusion.3
  769.6 64.6 %reduce-scatter.24.cloned.1.call-done = bf16[192,2304]{1,0:T(8,128)(2,1)} async-done(((bf16[768,2304]{1,0:T(8,128)(2,1)}), bf16[192,2304]{1,0:T(8,128)(2,1)}) %reduce-scatter.24.cloned.1.call-update) | async-done | bytes 884752 | tf_op jit(solution)/shard_map/reduce_scatter | solution.py:353
  834.2 87.7 %reduce-scatter.28.cloned.1.call-done = bf16[192,3072]{1,0:T(8,128)(2,1)} async-done(((bf16[768,3072]{1,0:T(8,128)(2,1)}), bf16[192,3072]{1,0:T(8,128)(2,1)}) %reduce-scatter.28.cloned.1.call-update) | async-done | bytes 1179664 | tf_op jit(solution)/shard_map/reduce_scatter | solution.py:365
  921.9 88.0 %reduce-scatter.30.cloned.1.call-done = bf16[192,3072]{1,0:T(8,128)(2,1)} async-done(((bf16[768,3072]{1,0:T(8,128)(2,1)}), bf16[192,3072]{1,0:T(8,128)(2,1)}) %reduce-scatter.30.cloned.1.call-update) | async-done | bytes 1179664 | tf_op jit(solution)/shard_map/reduce_scatter | solution.py:368
  1009.9 88.0 %reduce-scatter.32.cloned.1.call-done = bf16[768,768]{1,0:T(8,128)(2,1)} async-done(((bf16[3072,768]{1,0:T(8,128)(2,1)}), bf16[768,768]{1,0:T(8,128)(2,1)}) %reduce-scatter.32.cloned.1.call-update) | async-done | bytes 1179664 | tf_op jit(solution)/shard_map/reduce_scatter | solution.py:371
  1103.2 11.4 all-reduce.10
  1114.9 10.2 all-reduce.8
  1129.4 87.1 %all-reduce.14.cloned.1.call-done = (bf16[1,192,2304]{2,1,0:T(8,128)(2,1)}, bf16[1,192,768]{2,1,0:T(8,128)(2,1)}, bf16[1,192,3072]{2,1,0:T(8,128)(2,1)}, bf16[1,...) async-done(((bf16[1,192,2304]{2,1,0:T(8,128)(2,1)}, bf16[1,192,768]{2,1,0:T(8,128)(2,1)}, bf16[1,192,3072]{2,1,0:T(8,128)(2,1)}, bf16[1,192,3072]{2,1,0:T(8,128)(2,1)}, ...) | async-done | bytes 4718608 | tf_op jit(solution)/shard_map/psum | solution.py:382
  (759 shorter events, 274.0 us)
Async XLA Ops:
  7.3 75.3 %all-gather.15.cloned.1.call-start = ((), (), s32[]{:S(2)}) async-start(), calls=%async_computation.16 | async-start | bytes 4423680 | tf_op jit(solution)/shard_map/all_gather | solution.py:281
  8.0 131.0 %all-gather.17.cloned.1.call-start = ((), (), s32[]{:S(2)}) async-start(), calls=%async_computation.17 | async-start | bytes 1474560 | tf_op jit(solution)/shard_map/all_gather | solution.py:282
  8.7 207.4 %all-gather.19.cloned.1.call-start = ((), (), s32[]{:S(2)}) async-start(), calls=%async_computation.18 | async-start | bytes 5898240 | tf_op jit(solution)/shard_map/all_gather | solution.py:285
  9.5 296.0 %all-gather.21.cloned.1.call-start = ((), (), s32[]{:S(2)}) async-start(), calls=%async_computation.19 | async-start | bytes 5898240 | tf_op jit(solution)/shard_map/all_gather | solution.py:286
  10.1 384.7 %all-gather.23.cloned.1.call-start = ((), (), s32[]{:S(2)}) async-start(), calls=%async_computation.20 | async-start | bytes 5898240 | tf_op jit(solution)/shard_map/all_gather | solution.py:287
  10.6 541.4 %reduce-scatter.34.cloned.1.call-start = ((), (), s32[]{:S(2)}) async-start(), calls=%async_computation.21 | async-start | bytes 983040
  10.8 19.6 %collective-permute-start = (bf16[128,768]{1,0:T(8,128)(2,1)S(1)}, bf16[128,768]{1,0:T(8,128)(2,1)S(1)}, u32[]{:S(2)}, u32[]{:S(2)}) collective-permute-start(bf16[128,768]{1,0:T(8,128)(2,1)S(1)} %bitcast_select_fusion.2), channel_id=1, source_target_pairs={{0,16},{16,0},{1,17},{17,1},{2,18},{18,2},{3,19},{19,3},{4,20},{20... | collective-permute-start | bytes 589832 | tf_op jit(solution)/shard_map/ppermute | solution.py:21
  27.9 427.1 %copy-start.125 = (f32[768]{0:T(1024)}, f32[768]{0:T(1024)S(1)}, u32[]{:S(2)}) copy-start(f32[768]{0:T(1024)S(1)} %convert_element_type.460) | copy-start | bytes 9220
  399.6 3.8 collective-permute-start.1
  456.0 8.5 collective-permute-start.2
  527.9 49.1 %reduce-scatter.36.cloned.1.call-start = ((), (), s32[]{:S(2)}) async-start(), calls=%async_computation.22 | async-start | bytes 983040
  549.6 83.7 %reduce-scatter.38.cloned.1.call-start = ((), (), s32[]{:S(2)}) async-start(), calls=%async_computation.23 | async-start | bytes 983040
  581.8 11.6 collective-permute-start.3
  609.7 48.4 %reduce-scatter.40.cloned.1.call-start = ((), (), s32[]{:S(2)}) async-start(), calls=%async_computation.24 | async-start | bytes 983040
  615.2 98.1 %reduce-scatter.42.cloned.1.call-start = ((), (), s32[]{:S(2)}) async-start(), calls=%async_computation.25 | async-start | bytes 983040
  663.8 4.9 collective-permute-start.4
  687.4 48.2 %reduce-scatter.44.cloned.1.call-start = ((), (), s32[]{:S(2)}) async-start(), calls=%async_computation.26 | async-start | bytes 983040
  692.0 77.6 %reduce-scatter.26.cloned.1.call-start = ((), (), s32[]{:S(2)}) async-start(), calls=%async_computation.12 | async-start | bytes 1474560 | tf_op jit(solution)/shard_map/reduce_scatter | solution.py:356
  703.2 131.0 %reduce-scatter.24.cloned.1.call-start = ((), (), s32[]{:S(2)}) async-start(), calls=%async_computation.11 | async-start | bytes 4423680 | tf_op jit(solution)/shard_map/reduce_scatter | solution.py:353
  744.7 177.2 %reduce-scatter.28.cloned.1.call-start = ((), (), s32[]{:S(2)}) async-start(), calls=%async_computation.13 | async-start | bytes 5898240 | tf_op jit(solution)/shard_map/reduce_scatter | solution.py:365
  752.5 257.4 %reduce-scatter.30.cloned.1.call-start = ((), (), s32[]{:S(2)}) async-start(), calls=%async_computation.14 | async-start | bytes 5898240 | tf_op jit(solution)/shard_map/reduce_scatter | solution.py:368
  760.2 337.7 %reduce-scatter.32.cloned.1.call-start = ((), (), s32[]{:S(2)}) async-start(), calls=%async_computation.15 | async-start | bytes 5898240 | tf_op jit(solution)/shard_map/reduce_scatter | solution.py:371
  769.5 447.0 %all-reduce.14.cloned.1.call-start = ((), (), s32[]{:S(2)}) async-start(), calls=%async_computation.27 | async-start | bytes 9437184 | tf_op jit(solution)/shard_map/psum | solution.py:382
  1103.1 24.2 %collective-permute-start.5 = (bf16[128,768]{1,0:T(8,128)(2,1)}, bf16[128,768]{1,0:T(8,128)(2,1)S(1)}, u32[]{:S(2)}, u32[]{:S(2)}) collective-permute-start(bf16[128,768]{1,0:T(8,128)(2,1)} %fusion.150), channel_id=1, source_target_pairs={{0,16},{16,0},{1,17},{17,1},{2,18},{18,2},{3,19},{19,3},{4,20},{20... | collective-permute-start | bytes 589832 | tf_op jit(solution)/shard_map/ppermute | solution.py:21
  (225 other events, 3666.9 us)
Sparse Core Ops, SparseCore 0:
  9.7 72.8 all-gather.14
  84.1 40.6 all-gather.16
  126.4 89.6 all-gather.18
  217.6 87.8 all-gather.20
  306.9 87.8 all-gather.22
  528.0 23.9 reduce-scatter.33
  554.3 22.5 reduce-scatter.35
  609.9 23.3 reduce-scatter.37
  635.6 22.5 reduce-scatter.39
  687.5 22.5 reduce-scatter.41
  713.0 22.5 reduce-scatter.43
  738.3 28.4 reduce-scatter.25
  769.1 65.0 reduce-scatter.23
  836.3 85.5 reduce-scatter.27
  924.1 85.7 reduce-scatter.29
  1012.0 85.7 reduce-scatter.31
  1101.8 114.6 all-reduce.13
where the time goes:
time: 1240 us; the launch traced here: 1230 us
  waiting for transfers between devices  781 us (63%)
  blocking collectives  151 us (12%)
  matrix products  146 us (12%)
  local copies, waits for them, and re-layouts  73.1 us (6%)
  other arithmetic  54.3 us (4%)
  between operations  19.4 us (2%)
    reduce_scatter x1, waiting for transfers between devices, shards(): lax.psum_scatter(totals[6].astype(jnp.bfloat16), 'fsdp', scatter_dimensio...  88 us
    reduce_scatter x1, waiting for transfers between devices, shards(): lax.psum_scatter(totals[5].astype(jnp.bfloat16), 'fsdp', scatter_dimensio...  88 us
    reduce_scatter x1, waiting for transfers between devices, shards(): lax.psum_scatter(totals[4].astype(jnp.bfloat16), 'fsdp', scatter_dimensio...  87.7 us
    psum x1, waiting for transfers between devices, shards(): lax.psum(shares[0].astype(jnp.bfloat16), 'rep').astype(jnp.float32)  87.1 us
    all_gather x1, waiting for transfers between devices, shards(): lax.all_gather(w_up[0], 'fsdp', axis=0, tiled=True)  85 us
    all_gather x1, waiting for transfers between devices, shards(): lax.all_gather(w_down[0], 'fsdp', axis=0, tiled=True)  84.3 us
    all_gather x1, waiting for transfers between devices, shards(): lax.all_gather(w_gate[0], 'fsdp', axis=0, tiled=True)  75 us
    unnamed x23, waiting for transfers between devices  68.8 us
  transfers between devices with their start and end apart: 23, of which 14 were waited for; matrix products, arithmetic and copies ran while one was open for 13% of the time, Pallas kernels for 0%

commit v1 on v0

--- a/solution.py
+++ b/solution.py
@@ -25,6 +25,25 @@
     count = lax.axis_size(axis)
     initial, last = (max(0, -steps), min(count, count - steps))
     return lax.ppermute(value, axis, [(source, source + steps) for source in range(initial, last)])
+
+
+def gather_spread(block):
+    parts = lax.axis_size("rep")
+    size = block.shape[0] // parts
+    if block.ndim == 1 or block.shape[0] % parts or size % 16:
+        return lax.all_gather(block, "fsdp", axis=0, tiled=True)
+    part = lax.dynamic_slice_in_dim(block, lax.axis_index("rep") * size, size, 0)
+    return lax.all_gather(part, ("fsdp", "rep"), axis=0, tiled=True)
+
+
+def sum_spread(total):
+    parts = lax.axis_size("rep") * lax.axis_size("fsdp")
+    low = total.astype(jnp.bfloat16)
+    if total.ndim == 1 or total.shape[0] % parts or total.shape[0] // parts % 16:
+        share = lax.psum_scatter(low, "fsdp", scatter_dimension=0, tiled=True)
+        return lax.psum(share, "rep").astype(jnp.float32)
+    share = lax.psum_scatter(low, ("fsdp", "rep"), scatter_dimension=0, tiled=True)
+    return lax.all_gather(share, "rep", axis=0, tiled=True).astype(jnp.float32)
 
 
 def norm_rows(values, norm_gain, offset):
@@ -277,16 +296,11 @@
     model_width = tokens.shape[3]
     slot_count = row_count * lax.axis_size("fsdp")
     micro_count = lengths.shape[0]
-    weights = (
-        lax.all_gather(w_qkv[0], "fsdp", axis=0, tiled=True),
-        lax.all_gather(w_out[0], "fsdp", axis=0, tiled=True),
-        lax.all_gather(norm1_gain[0], "fsdp", axis=0, tiled=True),
-        lax.all_gather(norm1_bias[0], "fsdp", axis=0, tiled=True),
-        lax.all_gather(w_gate[0], "fsdp", axis=0, tiled=True),
-        lax.all_gather(w_up[0], "fsdp", axis=0, tiled=True),
-        lax.all_gather(w_down[0], "fsdp", axis=0, tiled=True),
-        lax.all_gather(norm2_gain[0], "fsdp", axis=0, tiled=True),
-        lax.all_gather(norm2_bias[0], "fsdp", axis=0, tiled=True),
+    weights = tuple(
+        gather_spread(value[0])
+        for value in (
+            w_qkv, w_out, norm1_gain, norm1_bias, w_gate, w_up, w_down, norm2_gain, norm2_bias,
+        )
     )
     own_tokens = tokens[0, 0]
     own_cotangent = cotangent[0, 0]
@@ -349,46 +363,7 @@
         if tick_index < micro_count:
             arriving = shifted(grad_low, "section", -1)
         totals = weight_grads if totals is None else jax.tree.map(jnp.add, totals, weight_grads)
-    shares = (
-        lax.psum_scatter(
-            totals[0].astype(jnp.bfloat16), "fsdp", scatter_dimension=0, tiled=True
-        ).astype(jnp.float32),
-        lax.psum_scatter(
-            totals[1].astype(jnp.bfloat16), "fsdp", scatter_dimension=0, tiled=True
-        ).astype(jnp.float32),
-        lax.psum_scatter(
-            totals[2].astype(jnp.bfloat16), "fsdp", scatter_dimension=0, tiled=True
-        ).astype(jnp.float32),
-        lax.psum_scatter(
-            totals[3].astype(jnp.bfloat16), "fsdp", scatter_dimension=0, tiled=True
-        ).astype(jnp.float32),
-        lax.psum_scatter(
-            totals[4].astype(jnp.bfloat16), "fsdp", scatter_dimension=0, tiled=True
-        ).astype(jnp.float32),
-        lax.psum_scatter(
-            totals[5].astype(jnp.bfloat16), "fsdp", scatter_dimension=0, tiled=True
-        ).astype(jnp.float32),
-        lax.psum_scatter(
-            totals[6].astype(jnp.bfloat16), "fsdp", scatter_dimension=0, tiled=True
-        ).astype(jnp.float32),
-        lax.psum_scatter(
-            totals[7].astype(jnp.bfloat16), "fsdp", scatter_dimension=0, tiled=True
-        ).astype(jnp.float32),
-        lax.psum_scatter(
-            totals[8].astype(jnp.bfloat16), "fsdp", scatter_dimension=0, tiled=True
-        ).astype(jnp.float32),
-    )
-    owned_total = (
-        lax.psum(shares[0].astype(jnp.bfloat16), "rep").astype(jnp.float32),
-        lax.psum(shares[1].astype(jnp.bfloat16), "rep").astype(jnp.float32),
-        lax.psum(shares[2].astype(jnp.bfloat16), "rep").astype(jnp.float32),
-        lax.psum(shares[3].astype(jnp.bfloat16), "rep").astype(jnp.float32),
-        lax.psum(shares[4].astype(jnp.bfloat16), "rep").astype(jnp.float32),
-        lax.psum(shares[5].astype(jnp.bfloat16), "rep").astype(jnp.float32),
-        lax.psum(shares[6].astype(jnp.bfloat16), "rep").astype(jnp.float32),
-        lax.psum(shares[7].astype(jnp.bfloat16), "rep").astype(jnp.float32),
-        lax.psum(shares[8].astype(jnp.bfloat16), "rep").astype(jnp.float32),
-    )
+    owned_total = tuple(sum_spread(total) for total in totals)
     outgoing = jnp.where(is_first, input_grads[2], layer_outputs[1])
     returned = partner(outgoing, "section", 0)
     output_rows = jnp.where(is_first, returned, layer_outputs[2])

time: 1240 us -> 1530 us (1.23)
  waiting for transfers between devices: 781 us -> 1050 us
    reduce_scatter x5, waiting for transfers between devices: 328 us -> 622 us  [sum_spread(): lax.psum_scatter(low, ('fsdp', 'rep'), scatter_dimension=0, tiled=True)]
    psum x1 -> x0, waiting for transfers between devices: 87.1 us -> none  [shards(): lax.psum(shares[0].astype(jnp.bfloat16), 'rep').astype(jnp.float32)]
    all_gather x5 -> x8, waiting for transfers between devices: 297 us -> 377 us  [the longest x5 296 us: gather_spread(): return lax.all_gather(part, ('fsdp', 'rep'), axis=0, tiled=True)]
    all_gather x0 -> x2, blocking collectives: none -> 22.2 us  [sum_spread(): return lax.all_gather(share, 'rep', axis=0, tiled=True).astype(jnp.float32)]
    unnamed x23 -> x25, waiting for transfers between devices: 68.8 us -> 53.1 us
    unnamed x477 -> x493, local copies, waits for them, and re-layouts: 40.1 us -> 37.1 us
  transfers between devices with their start and end apart: 23 -> 25, of which waited for: 14 -> 18; matrix products, arithmetic and copies ran while one was open for 13% -> 11% of each run, Pallas kernels for 0% -> 0%
where the time goes in v1:
time: 1530 us; the launch traced here: 1520 us
  waiting for transfers between devices  1050 us (69%)
  blocking collectives  164 us (11%)
  matrix products  141 us (9%)
  local copies, waits for them, and re-layouts  78.4 us (5%)
  other arithmetic  60.5 us (4%)
  between operations  19.6 us (1%)
    reduce_scatter x5, waiting for transfers between devices, sum_spread(): lax.psum_scatter(low, ('fsdp', 'rep'), scatter_dimension=0, tiled=True)  622 us
    all_gather x5, waiting for transfers between devices, gather_spread(): return lax.all_gather(part, ('fsdp', 'rep'), axis=0, tiled=True)  296 us
    all_gather x3, waiting for transfers between devices, sum_spread(): return lax.all_gather(share, 'rep', axis=0, tiled=True).astype(jnp.float32)  80.8 us
    all_gather x3, blocking collectives, layer_forward(): lax.all_gather(value_own, 'fsdp', axis=0, tiled=True)  54.7 us
    all_gather x3, blocking collectives, layer_forward(): lax.all_gather(key_own, 'fsdp', axis=0, tiled=True)  54.4 us
    unnamed x25, waiting for transfers between devices  53.1 us
    unnamed x493, local copies, waits for them, and re-layouts  37.1 us
  transfers between devices with their start and end apart: 25, of which 18 were waited for; matrix products, arithmetic and copies ran while one was open for 11% of the time, Pallas kernels for 0%

profile of v1, /device:TPU:0, one launch (start us, length us, event | category | flops | bytes accessed | tf_op | source)
XLA Modules:
  0.0 1523.5 jit_solution(277800244598810166)
XLA Ops:
  18.0 13.2 all-reduce.10
  34.9 50.7 %all-gather.24.cloned.1.call-done = bf16[1,768,2304]{2,1,0:T(8,128)(2,1)} async-done(((bf16[1,48,2304]{2,1,0:T(8,128)(2,1)}), bf16[1,768,2304]{2,1,0:T(8,128)(2,1)}) %all-gather.24.cloned.1.call-update) | async-done | bytes 3538960 | tf_op jit(solution)/shard_map/all_gather | solution.py:36
  88.3 18.8 %all_gather.61 = bf16[512,768]{1,0:T(8,128)(2,1)S(1)} all-gather(bf16[128,768]{1,0:T(8,128)(2,1)S(1)} %slice.188), channel_id=1, replica_groups=mesh['section'=2,'fsdp'=4,'rep'=4] {'fsdp'}, dimensions={0}, use_global_device_ids=true | all-gather | bytes 983040 | tf_op jit(solution)/shard_map/all_gather | solution.py:119
  112.4 20.3 %all_gather.62 = bf16[512,768]{1,0:T(8,128)(2,1)S(1)} all-gather(bf16[128,768]{1,0:T(8,128)(2,1)S(1)} %get-tuple-element.75), channel_id=1, replica_groups=mesh['section'=2,'fsdp'=4,'rep'=4] {'fsdp'}, dimensions={0}, use_global_device_ids=true | all-gather | bytes 983040 | tf_op jit(solution)/shard_map/all_gather | solution.py:118
  146.8 80.6 %all-gather.28.cloned.1.call-done = bf16[1,768,3072]{2,1,0:T(8,128)(2,1)} async-done(((bf16[1,48,3072]{2,1,0:T(8,128)(2,1)}), bf16[1,768,3072]{2,1,0:T(8,128)(2,1)}) %all-gather.28.cloned.1.call-update) | async-done | bytes 4718608 | tf_op jit(solution)/shard_map/all_gather | solution.py:36
  231.7 78.1 %all-gather.30.cloned.1.call-done = bf16[1,768,3072]{2,1,0:T(8,128)(2,1)} async-done(((bf16[1,48,3072]{2,1,0:T(8,128)(2,1)}), bf16[1,768,3072]{2,1,0:T(8,128)(2,1)}) %all-gather.30.cloned.1.call-update) | async-done | bytes 4718608 | tf_op jit(solution)/shard_map/all_gather | solution.py:36
  314.8 77.3 %all-gather.32.cloned.1.call-done = bf16[1,3072,768]{2,1,0:T(8,128)(2,1)} async-done(((bf16[1,192,768]{2,1,0:T(8,128)(2,1)}), bf16[1,3072,768]{2,1,0:T(8,128)(2,1)}) %all-gather.32.cloned.1.call-update) | async-done | bytes 4718608 | tf_op jit(solution)/shard_map/all_gather | solution.py:36
  400.6 18.8 %all_gather.71 = bf16[512,768]{1,0:T(8,128)(2,1)S(1)} all-gather(bf16[128,768]{1,0:T(8,128)(2,1)S(1)} %slice.187), channel_id=1, replica_groups=mesh['section'=2,'fsdp'=4,'rep'=4] {'fsdp'}, dimensions={0}, use_global_device_ids=true | all-gather | bytes 983040 | tf_op jit(solution)/shard_map/all_gather | solution.py:119
  429.9 17.7 %all_gather.72 = bf16[512,768]{1,0:T(8,128)(2,1)S(1)} all-gather(bf16[128,768]{1,0:T(8,128)(2,1)} %get-tuple-element.73), channel_id=1, replica_groups=mesh['section'=2,'fsdp'=4,'rep'=4] {'fsdp'}, dimensions={0}, use_global_device_ids=true | all-gather | bytes 983040 | tf_op jit(solution)/shard_map/all_gather | solution.py:118
  473.1 17.1 %all_gather.73 = bf16[512,768]{1,0:T(8,128)(2,1)} all-gather(bf16[128,768]{1,0:T(8,128)(2,1)S(1)} %slice.186), channel_id=1, replica_groups=mesh['section'=2,'fsdp'=4,'rep'=4] {'fsdp'}, dimensions={0}, use_global_device_ids=true | all-gather | bytes 983040 | tf_op jit(solution)/shard_map/all_gather | solution.py:119
  493.6 16.4 %all_gather.74 = bf16[512,768]{1,0:T(8,128)(2,1)S(1)} all-gather(bf16[128,768]{1,0:T(8,128)(2,1)S(1)} %get-tuple-element.71), channel_id=1, replica_groups=mesh['section'=2,'fsdp'=4,'rep'=4] {'fsdp'}, dimensions={0}, use_global_device_ids=true | all-gather | bytes 983040 | tf_op jit(solution)/shard_map/all_gather | solution.py:118
  564.8 13.2 reduce-scatter.36.cloned.1.call-done
  639.8 19.4 %reduce-scatter.40.cloned.1.call-done = bf16[128,768]{1,0:T(8,128)(2,1)} async-done(((bf16[512,768]{1,0:T(8,128)(2,1)}), bf16[128,768]{1,0:T(8,128)(2,1)}) %reduce-scatter.40.cloned.1.call-update) | async-done | bytes 196624
  723.5 10.1 reduce-scatter.44.cloned.1.call-done
  752.9 122.5 %reduce-scatter.28.cloned.1.call-done = bf16[48,3072]{1,0:T(8,128)(2,1)} async-done(((bf16[768,3072]{1,0:T(8,128)(2,1)}), bf16[48,3072]{1,0:T(8,128)(2,1)}) %reduce-scatter.28.cloned.1.call-update) | async-done | bytes 294928 | tf_op jit(solution)/shard_map/reduce_scatter | solution.py:45
  875.5 142.3 %reduce-scatter.30.cloned.1.call-done = bf16[48,3072]{1,0:T(8,128)(2,1)} async-done(((bf16[768,3072]{1,0:T(8,128)(2,1)}), bf16[48,3072]{1,0:T(8,128)(2,1)}) %reduce-scatter.30.cloned.1.call-update) | async-done | bytes 294928 | tf_op jit(solution)/shard_map/reduce_scatter | solution.py:45
  1022.1 10.9 all-reduce.9
  1045.5 100.3 %reduce-scatter.26.cloned.1.call-done = bf16[48,768]{1,0:T(8,128)(2,1)} async-done(((bf16[768,768]{1,0:T(8,128)(2,1)}), bf16[48,768]{1,0:T(8,128)(2,1)}) %reduce-scatter.26.cloned.1.call-update) | async-done | bytes 73744 | tf_op jit(solution)/shard_map/reduce_scatter | solution.py:45
  1156.1 127.8 %reduce-scatter.24.cloned.1.call-done = bf16[48,2304]{1,0:T(8,128)(2,1)} async-done(((bf16[768,2304]{1,0:T(8,128)(2,1)}), bf16[48,2304]{1,0:T(8,128)(2,1)}) %reduce-scatter.24.cloned.1.call-update) | async-done | bytes 221200 | tf_op jit(solution)/shard_map/reduce_scatter | solution.py:45
  1283.9 12.8 all_gather.75
  1296.6 128.9 %reduce-scatter.32.cloned.1.call-done = bf16[192,768]{1,0:T(8,128)(2,1)} async-done(((bf16[3072,768]{1,0:T(8,128)(2,1)}), bf16[192,768]{1,0:T(8,128)(2,1)}) %reduce-scatter.32.cloned.1.call-update) | async-done | bytes 294928 | tf_op jit(solution)/shard_map/reduce_scatter | solution.py:45
  1426.9 27.4 %all-gather.18.cloned.1.call-done = bf16[192,3072]{1,0:T(8,128)(2,1)} async-done(((bf16[48,3072]{1,0:T(8,128)(2,1)}), bf16[192,3072]{1,0:T(8,128)(2,1)}) %all-gather.18.cloned.1.call-update) | async-done | bytes 1179664 | tf_op jit(solution)/shard_map/all_gather | solution.py:46
  1457.3 26.6 %all-gather.20.cloned.1.call-done = bf16[192,3072]{1,0:T(8,128)(2,1)} async-done(((bf16[48,3072]{1,0:T(8,128)(2,1)}), bf16[192,3072]{1,0:T(8,128)(2,1)}) %all-gather.20.cloned.1.call-update) | async-done | bytes 1179664 | tf_op jit(solution)/shard_map/all_gather | solution.py:46
  1486.8 26.8 %all-gather.22.cloned.1.call-done = bf16[768,768]{1,0:T(8,128)(2,1)} async-done(((bf16[192,768]{1,0:T(8,128)(2,1)}), bf16[768,768]{1,0:T(8,128)(2,1)}) %all-gather.22.cloned.1.call-update) | async-done | bytes 1179664 | tf_op jit(solution)/shard_map/all_gather | solution.py:46
  (788 shorter events, 326.0 us)
Async XLA Ops:
  7.3 78.3 %all-gather.24.cloned.1.call-start = ((), (), s32[]{:S(2)}) async-start(), calls=%async_computation.19 | async-start | bytes 3760128 | tf_op jit(solution)/shard_map/all_gather | solution.py:36
  9.1 135.6 %all-gather.26.cloned.1.call-start = ((), (), s32[]{:S(2)}) async-start(), calls=%async_computation.20 | async-start | bytes 1253376 | tf_op jit(solution)/shard_map/all_gather | solution.py:36
  10.7 216.7 %all-gather.28.cloned.1.call-start = ((), (), s32[]{:S(2)}) async-start(), calls=%async_computation.21 | async-start | bytes 5013504 | tf_op jit(solution)/shard_map/all_gather | solution.py:36
  11.6 298.2 %all-gather.30.cloned.1.call-start = ((), (), s32[]{:S(2)}) async-start(), calls=%async_computation.22 | async-start | bytes 5013504 | tf_op jit(solution)/shard_map/all_gather | solution.py:36
  13.3 378.8 %all-gather.32.cloned.1.call-start = ((), (), s32[]{:S(2)}) async-start(), calls=%async_computation.23 | async-start | bytes 5013504 | tf_op jit(solution)/shard_map/all_gather | solution.py:36
  15.1 538.0 %reduce-scatter.34.cloned.1.call-start = ((), (), s32[]{:S(2)}) async-start(), calls=%async_computation.24 | async-start | bytes 983040
  15.2 19.6 %collective-permute-start = (bf16[128,768]{1,0:T(8,128)(2,1)S(1)}, bf16[128,768]{1,0:T(8,128)(2,1)S(1)}, u32[]{:S(2)}, u32[]{:S(2)}) collective-permute-start(bf16[128,768]{1,0:T(8,128)(2,1)S(1)} %bitcast_select_fusion.2), channel_id=1, source_target_pairs={{0,16},{16,0},{1,17},{17,1},{2,18},{18,2},{3,19},{19,3},{4,20},{20... | collective-permute-start | bytes 589832 | tf_op jit(solution)/shard_map/ppermute | solution.py:21
  459.5 9.1 collective-permute-start.2
  529.3 48.7 %reduce-scatter.36.cloned.1.call-start = ((), (), s32[]{:S(2)}) async-start(), calls=%async_computation.25 | async-start | bytes 983040
  551.0 83.2 %reduce-scatter.38.cloned.1.call-start = ((), (), s32[]{:S(2)}) async-start(), calls=%async_computation.26 | async-start | bytes 983040
  582.8 11.6 collective-permute-start.3
  610.8 48.4 %reduce-scatter.40.cloned.1.call-start = ((), (), s32[]{:S(2)}) async-start(), calls=%async_computation.27 | async-start | bytes 983040
  616.3 105.8 %reduce-scatter.42.cloned.1.call-start = ((), (), s32[]{:S(2)}) async-start(), calls=%async_computation.28 | async-start | bytes 983040
  664.7 4.8 collective-permute-start.4
  685.4 48.2 %reduce-scatter.44.cloned.1.call-start = ((), (), s32[]{:S(2)}) async-start(), calls=%async_computation.29 | async-start | bytes 983040
  688.9 186.6 %reduce-scatter.28.cloned.1.call-start = ((), (), s32[]{:S(2)}) async-start(), calls=%async_computation.13 | async-start | bytes 5013504 | tf_op jit(solution)/shard_map/reduce_scatter | solution.py:45
  696.9 320.9 %reduce-scatter.30.cloned.1.call-start = ((), (), s32[]{:S(2)}) async-start(), calls=%async_computation.15 | async-start | bytes 5013504 | tf_op jit(solution)/shard_map/reduce_scatter | solution.py:45
  704.6 441.2 %reduce-scatter.26.cloned.1.call-start = ((), (), s32[]{:S(2)}) async-start(), calls=%async_computation.12 | async-start | bytes 1253376 | tf_op jit(solution)/shard_map/reduce_scatter | solution.py:45
  712.1 571.8 %reduce-scatter.24.cloned.1.call-start = ((), (), s32[]{:S(2)}) async-start(), calls=%async_computation.11 | async-start | bytes 3760128 | tf_op jit(solution)/shard_map/reduce_scatter | solution.py:45
  743.3 682.2 %reduce-scatter.32.cloned.1.call-start = ((), (), s32[]{:S(2)}) async-start(), calls=%async_computation.17 | async-start | bytes 5013504 | tf_op jit(solution)/shard_map/reduce_scatter | solution.py:45
  752.9 701.4 %all-gather.18.cloned.1.call-start = ((), (), s32[]{:S(2)}) async-start(), calls=%async_computation.14 | async-start | bytes 1474560 | tf_op jit(solution)/shard_map/all_gather | solution.py:46
  875.5 608.4 %all-gather.20.cloned.1.call-start = ((), (), s32[]{:S(2)}) async-start(), calls=%async_computation.16 | async-start | bytes 1474560 | tf_op jit(solution)/shard_map/all_gather | solution.py:46
  1017.8 495.8 %all-gather.22.cloned.1.call-start = ((), (), s32[]{:S(2)}) async-start(), calls=%async_computation.18 | async-start | bytes 1474560 | tf_op jit(solution)/shard_map/all_gather | solution.py:46
  1021.9 22.6 %collective-permute-start.5 = (bf16[128,768]{1,0:T(8,128)(2,1)S(1)}, bf16[128,768]{1,0:T(8,128)(2,1)S(1)}, u32[]{:S(2)}, u32[]{:S(2)}) collective-permute-start(bf16[128,768]{1,0:T(8,128)(2,1)S(1)} %fusion.150), channel_id=1, source_target_pairs={{0,16},{16,0},{1,17},{17,1},{2,18},{18,2},{3,19},{19,3},{4,20},{20... | collective-permute-start | bytes 589832 | tf_op jit(solution)/shard_map/ppermute | solution.py:21
  (235 other events, 8835.9 us)
Sparse Core Ops, SparseCore 0:
  11.5 74.0 all-gather.23
  88.9 55.7 all-gather.25
  148.1 79.3 all-gather.27
  230.7 79.0 all-gather.29
  313.0 79.0 all-gather.31
  529.4 23.6 reduce-scatter.33
  555.4 22.5 reduce-scatter.35
  610.9 23.3 reduce-scatter.37
  636.5 22.5 reduce-scatter.39
  685.5 22.5 reduce-scatter.41
  711.0 22.5 reduce-scatter.43
  738.6 136.8 reduce-scatter.27
  881.5 136.3 reduce-scatter.29
  1023.0 122.7 reduce-scatter.25
  1150.8 133.0 reduce-scatter.23
  1288.9 136.5 reduce-scatter.31
  1427.4 26.8 all-gather.17
  1456.1 27.7 all-gather.19
  1485.9 27.7 all-gather.21

commit v2 on v0

--- a/solution.py
+++ b/solution.py
@@ -1,6 +1,11 @@
+import functools
+import types
+
 import jax
 import jax.numpy as jnp
 from jax import lax
+from jax.experimental import pallas as pl
+from jax.experimental.pallas import tpu as pltpu
 from jax.sharding import PartitionSpec as P
 
 HEADS = 12
@@ -9,6 +14,7 @@
 
 norm_eps = 1e-05
 masked_score = -1000000000.0
+VMEM_LIMIT = 62 * 2**20
 
 
 def partner(block, axis, distance):
@@ -408,9 +414,760 @@
     )
 
 
+MESH = pl.DeviceIdType.MESH
+BLOCK = 128
+LANES = 128
+QKV_PAD = 640
+NORM_ROW = 64
+
+
+def dot(left, right):
+    return jnp.dot(left, right, preferred_element_type=jnp.float32)
+
+
+def dot_rows(left, right):
+    return lax.dot_general(left, right, (((1,), (1,)), ((), ())), preferred_element_type=jnp.float32)
+
+
+def dot_cols(left, right):
+    return lax.dot_general(left, right, (((0,), (0,)), ((), ())), preferred_element_type=jnp.float32)
+
+
+def low(value):
+    return value.astype(jnp.bfloat16)
+
+
+def wide(value):
+    return value.astype(jnp.float32)
+
+
+def wait_for(ref, sem):
+    pltpu.make_async_copy(ref, ref, sem).wait()
+
+
+def turned(values):
+    lane = lax.broadcasted_iota(jnp.int32, values.shape, 1)
+    ahead = pltpu.roll(values, LANES - HEAD_DIM // 2, 1)
+    behind = pltpu.roll(values, HEAD_DIM // 2, 1)
+    return jnp.where(lane % HEAD_DIM < HEAD_DIM // 2, ahead, behind)
+
+
+def relay_scratch(width, hidden):
+    vm = pltpu.VMEM
+    bf, f32 = jnp.bfloat16, jnp.float32
+    slots = 4 * BLOCK
+    own = 2 * BLOCK
+    dma = pltpu.SemaphoreType.DMA
+    part = width // 4
+    share = part // 4
+    fpart = hidden // 4
+    fshare = fpart // 4
+    return dict(
+        wq=vm((2, width, QKV_PAD), bf), wo=vm((2, 256, width), bf), wgu=vm((2, width, 2 * fpart), bf),
+        wd=vm((2, fpart, width), bf),
+        x=vm((2, slots, width), bf), hid=vm((2, slots, width), bf), dfed=vm((2, slots, width), bf),
+        datt=vm((2, slots, width), bf),
+        q=vm((2, 3, slots, LANES), bf), k=vm((2, 3, slots, LANES), bf), v=vm((2, slots, 256), bf),
+        pr=vm((2, 3, slots, slots), bf), mix=vm((2, slots, 256), bf), gu=vm((2, slots, 2 * fpart), bf),
+        act=vm((2, slots, fpart), bf),
+        n1=vm((2, own, width), f32), n2=vm((2, own, width), f32),
+        i1=vm((2, own, LANES), f32), i2=vm((2, own, LANES), f32),
+        dgu=vm((slots, 2 * fpart), bf), dmix=vm((slots, 256), bf), dqkv=vm((slots, QKV_PAD), bf),
+        ds=vm((slots, slots), bf), dq=vm((slots, LANES), f32),
+        hidf=vm((own, width), f32), dres=vm((own, width), f32), dy=vm((own, width), f32),
+        mine=vm((own, width), f32), cot=vm((own, width), bf), outb=vm((own, width), bf), tgb=vm((own, width), bf),
+        sa=vm((2, 2, BLOCK, width), bf), ra=vm((2, 2, BLOCK, width), bf),
+        sb=vm((2, 2, BLOCK, width), bf), rb=vm((2, 2, BLOCK, width), bf),
+        par=vm((2, LANES, width), f32), ng=vm((2, LANES, width), f32),
+        r1q=vm((2, 3, part, QKV_PAD), bf), r1g=vm((2, 3, part, 2 * fpart), bf),
+        r1o=vm((2, 3, share, width), bf), r1d=vm((2, 3, fshare, width), bf),
+        s2q=vm((2, part, QKV_PAD), bf), s2g=vm((2, part, 2 * fpart), bf),
+        s2o=vm((2, share, width), bf), s2d=vm((2, fshare, width), bf),
+        r2q=vm((8, share, QKV_PAD), bf), r2g=vm((8, share, 2 * fpart), bf),
+        r2o=vm((2, share, width), bf), r2d=vm((2, fshare, width), bf),
+        s3q=vm((4, share, QKV_PAD), bf), s3g=vm((4, share, 2 * fpart), bf),
+        s3o=vm((share, width), bf), s3d=vm((fshare, width), bf),
+        tok_s=dma((2,)), tok_r=dma, cot_s=dma((2,)), cot_r=dma, xc_s=dma((2,)), xc_r=dma((2,)),
+        wz=dma((2, 4, 4)), wss=dma((2, 2)), wso=dma((2, 2, 2)), wfs=dma((2, 4)), wp=dma((2, 4)),
+        a_s=dma((2, 2)), a_r=dma((2, 2)), b_s=dma((2, 2)), b_r=dma((2, 2)), c_s=dma((8, 2)), c_r=dma((8, 2)),
+        s1s=dma((2, 4)), s1r=dma((2, 4)), s2s=dma((2, 4)), s2r=dma((4,)), s3s=dma((4,)), s3r=dma((4,)),
+        o_s=dma((2,)), o_r=dma((2,)),
+    )
+
+
+def relay_kernel(names, length_ref, cos_ref, sin_ref, tok_ref, cot_ref, wq_ref, wo_ref, wg_ref, wu_ref, wd_ref,
+                 out_ref, tg_ref, oq_ref, oo_ref, og_ref, od_ref, *scratch):
+    m = types.SimpleNamespace(**dict(zip(names, scratch)))
+    width = tok_ref.shape[3]
+    slots = 4 * BLOCK
+    part = width // 4
+    share = part // 4
+    fpart = wd_ref.shape[1]
+    fshare = fpart // 4
+    s, z, r = lax.axis_index("section"), lax.axis_index("fsdp"), lax.axis_index("rep")
+    zp, zh = z % 2, z // 2
+    r0, r1 = r % 2, r // 2
+    t = 2 * zp + s
+    other = 1 - s
+
+    def mixed(low_bit, high_bit, k):
+        a = 1 - low_bit if k & 1 else low_bit
+        b = 1 - high_bit if k & 2 else high_bit
+        return a + 2 * b
+
+    z_of = [mixed(zp, zh, k) for k in range(4)]
+    r_of = [mixed(r0, r1, k) for k in range(4)]
+    zp_of = [zp, 1 - zp, zp, 1 - zp]
+    across = (other, z, r)
+    along = (s, z_of[1], r)
+
+    def remote(src, dst, send, recv, device):
+        return pltpu.make_async_remote_copy(
+            src_ref=src, dst_ref=dst, send_sem=send, recv_sem=recv, device_id=device, device_id_type=MESH)
+
+    def rows(start, size):
+        return pl.ds(pl.multiple_of(start, 16), size)
+
+    barrier = pltpu.get_barrier_semaphore()
+    greeted = [(other, z_of[0], r)] + [(c, z_of[k], r) for k in (1, 2, 3) for c in (0, 1)]
+    greeted += [(s, z, r_of[k]) for k in (1, 2, 3)]
+    for device in greeted:
+        pl.semaphore_signal(barrier, inc=1, device_id=device, device_id_type=MESH)
+    pl.semaphore_wait(barrier, len(greeted))
+
+    def scatter_rows(src, dst, send, recv, step):
+        for i in range(2):
+            target = 2 * s + i
+            is_self = (target == z) & (s == zp)
+
+            @pl.when(is_self)
+            def _():
+                if step == "start":
+                    pltpu.make_async_copy(src, dst, recv).start()
+
+            @pl.when(jnp.logical_not(is_self))
+            def _():
+                copy = remote(src, dst, send.at[i], recv, (zp, target, r))
+                if step == "start":
+                    copy.start()
+                else:
+                    copy.wait_send()
+
+    tok_args = (tok_ref.at[0, 0], m.x.at[0, rows(z * BLOCK, BLOCK)], m.tok_s, m.tok_r)
+    cot_args = (cot_ref.at[0, 0], m.cot.at[rows(zh * BLOCK, BLOCK)], m.cot_s, m.cot_r)
+    scatter_rows(*tok_args, "start")
+
+    Q, G, O, D = range(4)
+    weight = [m.wq, m.wgu, m.wo, m.wd]
+    count = [share, share, share, fshare]
+
+    def source_fan(l, kind):
+        for k in range(4):
+            size = part if k == 0 else share
+            start = 0 if k == 0 else r * share
+            here = rows(z * part + start, size)
+            for c in range(2):
+                target = 2 * zp_of[k] + c
+                device = (c, z_of[k], r)
+                if kind == Q:
+                    pairs = [(wq_ref.at[target, rows(start, size)], m.wq.at[l, here])]
+                else:
+                    cols = pl.ds(pl.multiple_of(target * fpart, LANES), fpart)
+                    pairs = [
+                        (wg_ref.at[0, rows(start, size), cols], m.wgu.at[l, here, pl.ds(0, fpart)]),
+                        (wu_ref.at[0, rows(start, size), cols], m.wgu.at[l, here, pl.ds(fpart, fpart)]),
+                    ]
+                for src, dst in pairs:
+                    if k == 0 and c == l:
+                        pltpu.make_async_copy(src, dst, m.wz.at[l, kind, k]).start()
+                    else:
+                        remote(src, dst, m.wss.at[l, kind], m.wz.at[l, kind, k], device).start()
+
+    def source_own(l, kind, step):
+        ref = wo_ref if kind == O else wd_ref
+        n = count[kind]
+        for i in range(2):
+            target = zh + 2 * i
+            own = target == z
+
+            def send(src, dst):
+                copy = remote(src, dst, m.wso.at[l, kind - O, i], m.wz.at[l, kind, 0], (zp, target, r))
+                if step == "start":
+                    copy.start()
+                else:
+                    copy.wait_send()
+
+            @pl.when(own & (zp == l))
+            def _():
+                if step == "start":
+                    pltpu.make_async_copy(
+                        ref.at[0], weight[kind].at[l, pl.ds(0, 4 * n)], m.wz.at[l, kind, 0]).start()
+
+            @pl.when(own & (zp != l))
+            def _():
+                send(ref.at[0], weight[kind].at[l, pl.ds(0, 4 * n)])
+
+            @pl.when(jnp.logical_not(own))
+            def _():
+                send(ref.at[0, rows(r * n, n)], weight[kind].at[l, rows(r * n, n)])
+
+    def source(l):
+        @pl.when(s == l)
+        def _():
+            source_fan(l, Q)
+            source_own(l, O, "start")
+            source_fan(l, G)
+            source_own(l, D, "start")
+
+    def source_done(l):
+        @pl.when(s == l)
+        def _():
+            size = 6 * share + part
+            wait_for(m.wq.at[l, pl.ds(0, size)], m.wss.at[l, Q])
+            wait_for(m.wgu.at[l, pl.ds(0, size)], m.wss.at[l, G])
+            source_own(l, O, "wait")
+            source_own(l, D, "wait")
+
+    def pass_on(l, kind, here):
+        for k in (1, 2, 3):
+            block = weight[kind].at[l, here]
+            remote(block, block, m.wfs.at[l, kind], m.wp.at[l, kind], (s, z, r_of[k])).start()
+
+    def forward(l, kind):
+        n = count[kind]
+        if kind in (Q, G):
+            for k in (1, 2, 3):
+                here = rows(z_of[k] * part + r * n, n)
+                wait_for(weight[kind].at[l, here], m.wz.at[l, kind, k])
+                pass_on(l, kind, here)
+        else:
+            @pl.when(t != z)
+            def _():
+                here = rows(r * n, n)
+                wait_for(weight[kind].at[l, here], m.wz.at[l, kind, 0])
+                pass_on(l, kind, here)
+
+    def need(l, kind):
+        n = count[kind]
+        if kind in (Q, G):
+            wait_for(weight[kind].at[l, rows(z * part, part)], m.wz.at[l, kind, 0])
+            wait_for(weight[kind].at[l, pl.ds(0, 9 * n)], m.wp.at[l, kind])
+        else:
+            @pl.when(t != z)
+            def _():
+                wait_for(weight[kind].at[l, pl.ds(0, 3 * n)], m.wp.at[l, kind])
+
+            @pl.when(t == z)
+            def _():
+                wait_for(weight[kind].at[l, pl.ds(0, 4 * n)], m.wz.at[l, kind, 0])
+
+    def forward_done(l, kind):
+        n = count[kind]
+        if kind in (Q, G):
+            wait_for(weight[kind].at[l, pl.ds(0, 9 * n)], m.wfs.at[l, kind])
+        else:
+            @pl.when(t != z)
+            def _():
+                wait_for(weight[kind].at[l, pl.ds(0, 3 * n)], m.wfs.at[l, kind])
+
+    def own_rows(j):
+        return rows((2 * j + s) * BLOCK, BLOCK)
+
+    def other_rows(j):
+        return rows((2 * j + other) * BLOCK, BLOCK)
+
+    def kept(j):
+        return pl.ds(j * BLOCK, BLOCK)
+
+    def send_partial(e, j, left, right, multiply):
+        p = e % 2
+        m.sa[p, j] = low(multiply(left[other_rows(j)], right))
+        copy = remote(m.sa.at[p, j], m.ra.at[p, j], m.a_s.at[p, j], m.a_r.at[p, j], across)
+        copy.start()
+        m.mine[kept(j)] = multiply(left[own_rows(j)], right)
+        return copy
+
+    def send_sum(e, j, copy):
+        p = e % 2
+        copy.wait()
+        m.sb[p, j] = low(m.mine[kept(j)] + wide(m.ra[p, j]))
+        copy = remote(m.sb.at[p, j], m.rb.at[p, j], m.b_s.at[p, j], m.b_r.at[p, j], along)
+        copy.start()
+        return copy
+
+    def summed(e, j, copy):
+        p = e % 2
+        copy.wait()
+        return wide(m.sb[p, j]) + wide(m.rb[p, j])
+
+    def share_rows(e, j, ref):
+        block = ref.at[own_rows(j)]
+        copy = remote(block, block, m.c_s.at[e, j], m.c_r.at[e, j], across)
+        copy.start()
+        return copy
+
+    lane = lax.broadcasted_iota(jnp.int32, (BLOCK, LANES), 1)
+    lane2 = lax.broadcasted_iota(jnp.int32, (BLOCK, 256), 1)
+    length = length_ref[0]
+    live_keys = lax.broadcasted_iota(jnp.int32, (BLOCK, slots), 1) < length
+    scale = HEAD_DIM ** (-0.5)
+
+    def param(l, i):
+        return m.par[l, pl.ds(NORM_ROW + i, 1), :]
+
+    def read_params(l):
+        for i in range(width // LANES):
+            cols = pl.ds(i * LANES, LANES)
+            m.par[l, :, cols] = jnp.transpose(wide(m.wq[l, cols, pl.ds(QKV_PAD - LANES, LANES)]))
+
+    def project(l, j):
+        @pl.loop(2 * j, 2 * j + 2)
+        def _(i):
+            here = rows(i * BLOCK, BLOCK)
+            joined = dot(m.x[l, here], m.wq[l])
+            cosine, sine = cos_ref[here], sin_ref[here]
+            for h in range(3):
+                values = joined[:, h * LANES:(h + 1) * LANES]
+                values = values * cosine + turned(values) * sine
+                m.q[l, h, here] = low(jnp.where(lane < HEAD_DIM, values, 0.0))
+                m.k[l, h, here] = low(pltpu.roll(values, HEAD_DIM, 1))
+            m.v[l, here] = low(jnp.where(lane2 < 3 * HEAD_DIM, joined[:, 3 * LANES:], 0.0))
+
+    def attend(l):
+        @pl.loop(0, slots // BLOCK)
+        def _(i):
+            here = rows(i * BLOCK, BLOCK)
+            total = jnp.zeros((BLOCK, 256), jnp.float32)
+            for h in range(3):
+                scores = dot_rows(m.q[l, h, here], m.k[l, h]) * scale
+                scores = jnp.where(live_keys, scores, masked_score)
+                top = jnp.max(scores, axis=-1, keepdims=True)
+                weights = jnp.exp(scores - top)
+                weights = low(weights / jnp.sum(weights, axis=-1, keepdims=True))
+                m.pr[l, h, here] = weights
+                inside = lane2 // HEAD_DIM == h
+                total = jnp.where(inside, dot(weights, m.v[l]), total)
+            m.mix[l, here] = low(total)
+
+    def normed(values):
+        centre = values - jnp.mean(values, axis=-1, keepdims=True)
+        inverse = lax.rsqrt(jnp.mean(centre * centre, axis=-1, keepdims=True) + norm_eps)
+        return centre * inverse, inverse
+
+    def finish_attention(e, l, j, copy):
+        values = wide(m.x[l, own_rows(j)]) + summed(e, j, copy)
+        norm, inverse = normed(values)
+        m.n1[l, kept(j)] = norm
+        m.i1[l, kept(j)] = jnp.broadcast_to(inverse, (BLOCK, LANES))
+        hidden = norm * param(l, 0) + param(l, 1)
+        m.hidf[kept(j)] = hidden
+        m.hid[l, own_rows(j)] = low(hidden)
+        return share_rows(l, j, m.hid.at[l])
+
+    def feed(l, j):
+        @pl.loop(2 * j, 2 * j + 2)
+        def _(i):
+            here = rows(i * BLOCK, BLOCK)
+            rows_in = m.hid[l, here]
+            gate = dot(rows_in, m.wgu[l, :, pl.ds(0, fpart)])
+            up = dot(rows_in, m.wgu[l, :, pl.ds(fpart, fpart)])
+            m.gu[l, here, pl.ds(0, fpart)] = low(gate)
+            m.gu[l, here, pl.ds(fpart, fpart)] = low(up)
+            m.act[l, here] = low(gate * jax.nn.sigmoid(gate) * up)
+
+    def finish_feed(e, l, j, copy):
+        values = m.hidf[kept(j)] + summed(e, j, copy)
+        norm, inverse = normed(values)
+        m.n2[l, kept(j)] = norm
+        m.i2[l, kept(j)] = jnp.broadcast_to(inverse, (BLOCK, LANES))
+        result = low(norm * param(l, 2) + param(l, 3))
+        if l == 0:
+            m.x[1, own_rows(j)] = result
+            return share_rows(2, j, m.x.at[1])
+        m.outb[kept(j)] = result
+        return None
+
+    counts = jnp.where(zp == 0, 1.0, 0.0)
+
+    def add_norm_grads(l, i, dy, norm):
+        for k, value in enumerate((dy * norm, dy)):
+            at = pl.ds(NORM_ROW + i + k, 1)
+            m.ng[l, at, :] += jnp.sum(value, axis=0, keepdims=True) * counts
+
+    def norm_grad(dy, norm, inverse, gain):
+        scaled = dy * gain
+        return inverse * (
+            scaled - jnp.mean(scaled, axis=-1, keepdims=True)
+            - norm * jnp.mean(scaled * norm, axis=-1, keepdims=True))
+
+    def back_second(l, j):
+        dy = m.dy[kept(j)]
+        norm = m.n2[l, kept(j)]
+        add_norm_grads(l, 2, dy, norm)
+        grad = norm_grad(dy, norm, m.i2[l, kept(j), pl.ds(0, 1)], param(l, 2))
+        m.dres[kept(j)] = grad
+        m.dfed[l, own_rows(j)] = low(grad)
+        return share_rows(3 + l, j, m.dfed.at[l])
+
+    def back_feed(l, j):
+        @pl.loop(2 * j, 2 * j + 2)
+        def _(i):
+            here = rows(i * BLOCK, BLOCK)
+            dact = dot_rows(m.dfed[l, here], m.wd[l])
+            gate = wide(m.gu[l, here, pl.ds(0, fpart)])
+            up = wide(m.gu[l, here, pl.ds(fpart, fpart)])
+            sig = jax.nn.sigmoid(gate)
+            m.dgu[here, pl.ds(0, fpart)] = low(dact * up * sig * (1.0 + gate * (1.0 - sig)))
+            m.dgu[here, pl.ds(fpart, fpart)] = low(dact * gate * sig)
+
+    def back_first(e, l, j, copy):
+        dhidden = m.dres[kept(j)] + summed(e, j, copy)
+        norm = m.n1[l, kept(j)]
+        add_norm_grads(l, 0, dhidden, norm)
+        grad = norm_grad(dhidden, norm, m.i1[l, kept(j), pl.ds(0, 1)], param(l, 0))
+        m.dres[kept(j)] = grad
+        m.datt[l, own_rows(j)] = low(grad)
+        return share_rows(5 + l, j, m.datt.at[l])
+
+    def back_mix(l, j):
+        @pl.loop(2 * j, 2 * j + 2)
+        def _(i):
+            here = rows(i * BLOCK, BLOCK)
+            m.dmix[here] = low(dot_rows(m.datt[l, here], m.wo[l]))
+
+    def back_attend(l):
+        for h in range(3):
+            inside = lane2 // HEAD_DIM == h
+
+            @pl.loop(0, slots // BLOCK)
+            def _(i):
+                here = rows(i * BLOCK, BLOCK)
+                grad = m.dmix[here]
+                grad = jnp.where(inside, grad, jnp.zeros_like(grad))
+                dprobs = dot_rows(grad, m.v[l])
+                probs = wide(m.pr[l, h, here])
+                centre = jnp.sum(dprobs * probs, axis=-1, keepdims=True)
+                dscores = low(probs * (dprobs - centre))
+                m.ds[here] = dscores
+                m.dq[here] = dot(dscores, m.k[l, h]) * scale
+
+            @pl.loop(0, slots // BLOCK)
+            def _(i):
+                here = rows(i * BLOCK, BLOCK)
+                cols = pl.ds(pl.multiple_of(i * BLOCK, LANES), BLOCK)
+                dkey = dot_cols(m.ds[:, cols], m.q[l, h]) * scale
+                values = jnp.where(lane < HEAD_DIM, m.dq[here], pltpu.roll(dkey, HEAD_DIM, 1))
+                values = values * cos_ref[here] - turned(values) * sin_ref[here]
+                m.dqkv[here, pl.ds(h * LANES, LANES)] = low(values)
+                dvalue = low(dot_cols(m.pr[l, h, :, cols], m.dmix[...]))
+                before = jnp.zeros_like(dvalue) if h == 0 else m.dqkv[here, pl.ds(3 * LANES, 256)]
+                m.dqkv[here, pl.ds(3 * LANES, 256)] = jnp.where(inside, dvalue, before)
+
+    def weight_grad(l, kind):
+        left, right = (
+            (m.x.at[l], m.dqkv), (m.hid.at[l], m.dgu), (m.mix.at[l], m.datt.at[l]),
+            (m.act.at[l], m.dfed.at[l]),
+        )[kind]
+
+        @pl.loop(0, left.shape[1] // LANES)
+        def _(i):
+            cols = pl.ds(pl.multiple_of(i * LANES, LANES), LANES)
+            grad = dot_cols(left[:, cols], right[...])
+            if kind == Q:
+                tail = grad[:, QKV_PAD - LANES:] + jnp.transpose(m.ng[l, :, cols])
+                weight[kind][l, cols, pl.ds(0, QKV_PAD - LANES)] = low(grad[:, :QKV_PAD - LANES])
+                weight[kind][l, cols, pl.ds(QKV_PAD - LANES, LANES)] = low(tail)
+            else:
+                weight[kind][l, cols] = low(grad)
+
+    first_in = [m.r1q, m.r1g, m.r1o, m.r1d]
+    second_out = [m.s2q, m.s2g, m.s2o, m.s2d]
+    second_in = [m.r2q, m.r2g, m.r2o, m.r2d]
+    third_out = [m.s3q, m.s3g, m.s3o, m.s3d]
+    final = [oq_ref, og_ref, oo_ref, od_ref]
+
+    def spread_plane(l, kind):
+        n = count[kind]
+        for k in (1, 2, 3):
+            for b in range(4 if kind in (Q, G) else 1):
+                start = (b * part if kind in (Q, G) else 0) + r_of[k] * n
+                remote(
+                    weight[kind].at[l, rows(start, n)], first_in[kind].at[l, k - 1, pl.ds(b * n, n)],
+                    m.s1s.at[l, kind], m.s1r.at[l, kind], (s, z, r_of[k])).start()
+
+    def spread_line(l, kind):
+        n = count[kind]
+        wait_for(first_in[kind].at[l], m.s1r.at[l, kind])
+        for b in range(4 if kind in (Q, G) else 1):
+            start = (b * part if kind in (Q, G) else 0) + r * n
+            total = wide(weight[kind][l, rows(start, n)])
+            for k in range(3):
+                total += wide(first_in[kind][l, k, pl.ds(b * n, n)])
+            second_out[kind][l, pl.ds(b * n, n)] = low(total)
+        if kind in (Q, G):
+            slot = 2 * z + s
+            for k in range(4):
+                src = second_out[kind].at[l, rows(z_of[k] * n, n)]
+                dst = second_in[kind].at[slot]
+                if k == 0:
+                    @pl.when(s == l)
+                    def _():
+                        pltpu.make_async_copy(src, dst, m.s2r.at[kind]).start()
+
+                    @pl.when(s != l)
+                    def _():
+                        remote(src, dst, m.s2s.at[l, kind], m.s2r.at[kind], across).start()
+                else:
+                    remote(src, dst, m.s2s.at[l, kind], m.s2r.at[kind], (l, z_of[k], r)).start()
+        else:
+            src, dst = second_out[kind].at[l], second_in[kind].at[zh]
+            is_self = (t == z) & (s == l)
+
+            @pl.when(is_self)
+            def _():
+                pltpu.make_async_copy(src, dst, m.s2r.at[kind]).start()
+
+            @pl.when(jnp.logical_not(is_self))
+            def _():
+                remote(src, dst, m.s2s.at[l, kind], m.s2r.at[kind], (l, t, r)).start()
+
+    def line_done(l, kind):
+        wait_for(first_in[kind].at[l], m.s1s.at[l, kind])
+        n = count[kind]
+        if kind in (Q, G):
+            @pl.when(s == l)
+            def _():
+                wait_for(second_out[kind].at[l, pl.ds(0, 3 * n)], m.s2s.at[l, kind])
+
+            @pl.when(s != l)
+            def _():
+                wait_for(second_out[kind].at[l], m.s2s.at[l, kind])
+        else:
+            @pl.when(jnp.logical_not((t == z) & (s == l)))
+            def _():
+                wait_for(second_out[kind].at[l], m.s2s.at[l, kind])
+
+    def finish(kind):
+        n = count[kind]
+        wait_for(second_in[kind], m.s2r.at[kind])
+        if kind in (Q, G):
+            for b in range(4):
+                near = 2 * (b // 2) + b % 2
+                total = wide(second_in[kind][near]) + wide(second_in[kind][near + 4])
+                third_out[kind][b] = low(total)
+            dst = final[kind].at[:, rows(r * n, n), :]
+        else:
+            third_out[kind][...] = low(wide(second_in[kind][0]) + wide(second_in[kind][1]))
+            dst = final[kind].at[rows(r * n, n), :]
+        for k in (1, 2, 3):
+            remote(third_out[kind], dst, m.s3s.at[kind], m.s3r.at[kind], (s, z, r_of[k])).start()
+        pltpu.make_async_copy(third_out[kind], dst, m.s3r.at[kind]).start()
+
+    def finish_done(kind):
+        wait_for(final[kind], m.s3r.at[kind])
+        wait_for(first_in[kind].at[0], m.s3s.at[kind])
+
+    def send_rows(i, src, dst, step):
+        block = src.at[rows(zp * BLOCK, BLOCK)]
+        is_self = (zh == s) & (t == z)
+
+        @pl.when(is_self)
+        def _():
+            if step == "start":
+                pltpu.make_async_copy(block, dst, m.o_r.at[i]).start()
+
+        @pl.when(jnp.logical_not(is_self))
+        def _():
+            copy = remote(block, dst, m.o_s.at[i], m.o_r.at[i], (zh, t, r))
+            if step == "start":
+                copy.start()
+            else:
+                copy.wait_send()
+
+        if step == "wait":
+            wait_for(dst, m.o_r.at[i])
+
+    source(0)
+    scatter_rows(*cot_args, "start")
+    for l in range(2):
+        m.wo[l, pl.ds(part, 256 - part)] = jnp.zeros((256 - part, width), jnp.bfloat16)
+        m.ng[l] = jnp.zeros((LANES, width), jnp.float32)
+    wait_for(m.x.at[0, pl.ds(0, 2 * BLOCK)], m.tok_r)
+    halves = []
+    for j in range(2):
+        block = m.x.at[0, own_rows(j)]
+        copy = remote(block, block, m.xc_s.at[j], m.xc_r.at[j], across)
+        copy.start()
+        halves.append(copy)
+    forward(0, Q)
+    need(0, Q)
+    read_params(0)
+    for j in range(2):
+        halves[j].wait()
+        project(0, j)
+    forward(0, O)
+    forward(0, G)
+    source(1)
+    e = 0
+    for l in range(2):
+        attend(l)
+        if l == 0:
+            forward(0, D)
+        need(l, O)
+        a = [send_partial(e, j, m.mix.at[l], m.wo[l], dot) for j in range(2)]
+        b = [send_sum(e, j, a[j]) for j in range(2)]
+        if l == 0:
+            forward(1, Q)
+            forward(1, O)
+        c0 = finish_attention(e, l, 0, b[0])
+        need(l, G)
+        need(l, D)
+        c0.wait()
+        feed(l, 0)
+        a0 = send_partial(e + 1, 0, m.act.at[l], m.wd[l], dot)
+        c1 = finish_attention(e, l, 1, b[1])
+        b0 = send_sum(e + 1, 0, a0)
+        c1.wait()
+        feed(l, 1)
+        a1 = send_partial(e + 1, 1, m.act.at[l], m.wd[l], dot)
+        b1 = send_sum(e + 1, 1, a1)
+        if l == 0:
+            forward(1, G)
+            forward(1, D)
+            need(1, Q)
+            read_params(1)
+        e += 1
+        for j, copy in ((0, b0), (1, b1)):
+            done = finish_feed(e, l, j, copy)
+            if l == 0:
+                done.wait()
+                project(1, j)
+        e += 1
+    send_rows(0, m.outb, out_ref.at[0, 0], "start")
+    for l in range(2):
+        source_done(l)
+        for kind in (Q, O, G, D):
+            forward_done(l, kind)
+    wait_for(m.cot, m.cot_r)
+    for j in range(2):
+        slot = (2 * j + s) * BLOCK + lax.broadcasted_iota(jnp.int32, (BLOCK, width), 0)
+        m.dy[kept(j)] = jnp.where(slot < length, wide(m.cot[kept(j)]), 0.0)
+    for l in (1, 0):
+        c = [back_second(l, j) for j in range(2)]
+        a = []
+        for j in range(2):
+            c[j].wait()
+            back_feed(l, j)
+            a.append(send_partial(e, j, m.dgu, m.wgu[l], dot_rows))
+        b0 = send_sum(e, 0, a[0])
+        weight_grad(l, D)
+        spread_plane(l, D)
+        b1 = send_sum(e, 1, a[1])
+        weight_grad(l, G)
+        spread_plane(l, G)
+        c = [back_first(e, l, j, copy) for j, copy in ((0, b0), (1, b1))]
+        e += 1
+        for j in range(2):
+            c[j].wait()
+            back_mix(l, j)
+        back_attend(l)
+        a = [send_partial(e, j, m.dqkv, m.wq[l], dot_rows) for j in range(2)]
+        b0 = send_sum(e, 0, a[0])
+        weight_grad(l, O)
+        spread_plane(l, O)
+        b1 = send_sum(e, 1, a[1])
+        weight_grad(l, Q)
+        spread_plane(l, Q)
+        for j, copy in ((0, b0), (1, b1)):
+            result = low(m.dres[kept(j)] + summed(e, j, copy))
+            if l == 1:
+                m.dy[kept(j)] = wide(result)
+            else:
+                m.tgb[kept(j)] = result
+        e += 1
+    send_rows(1, m.tgb, tg_ref.at[0, 0], "start")
+    for l in (1, 0):
+        for kind in (D, G, O, Q):
+            spread_line(l, kind)
+
+        @pl.when(s == l)
+        def _():
+            for kind in (D, G, O, Q):
+                finish(kind)
+    for kind in (D, G, O, Q):
+        finish_done(kind)
+        for l in (1, 0):
+            line_done(l, kind)
+    scatter_rows(*tok_args, "wait")
+    scatter_rows(*cot_args, "wait")
+    send_rows(0, m.outb, out_ref.at[0, 0], "wait")
+    send_rows(1, m.tgb, tg_ref.at[0, 0], "wait")
+
+
+def relay(tokens, lengths, cotangent, w_qkv, w_out, norm1_gain, norm1_bias, w_gate, w_up, w_down, norm2_gain, norm2_bias):
+    bf = jnp.bfloat16
+    part, width = w_qkv.shape[1], tokens.shape[3]
+    hidden = w_gate.shape[2]
+    slots = 4 * BLOCK
+    cosine, sine = rotary_tables(0, slots)
+    sign = jnp.where(jnp.arange(HEAD_DIM) < HEAD_DIM // 2, -1.0, 1.0)
+    cosine = jnp.tile(cosine[:, 0], (1, 2))
+    sine = jnp.tile(sine[:, 0] * sign, (1, 2))
+    length = lax.dynamic_slice_in_dim(lengths[:, 0], lax.axis_index("fsdp") // 2, 1, 0)
+    query, key, value = jnp.split(w_qkv[0], 3, axis=1)
+    heads = (part, 4, 3, HEAD_DIM)
+    joined = jnp.stack([query.reshape(heads), key.reshape(heads)], axis=3).reshape(part, 4, 6 * HEAD_DIM)
+    norms = jnp.stack([norm1_gain[0], norm1_bias[0], norm2_gain[0], norm2_bias[0]], axis=1)
+    norms = jnp.broadcast_to(jnp.pad(norms, ((0, 0), (0, HEAD_DIM - 4)))[:, None], (part, 4, HEAD_DIM))
+    packed = jnp.concatenate([joined, value.reshape(part, 4, 3 * HEAD_DIM), norms], axis=2).transpose(1, 0, 2)
+    scratch = relay_scratch(width, hidden)
+    any_space, vmem = pl.BlockSpec(memory_space=pl.ANY), pl.BlockSpec(memory_space=pltpu.VMEM)
+    fpart = hidden // 4
+    outs = pl.pallas_call(
+        functools.partial(relay_kernel, tuple(scratch)),
+        out_shape=(
+            jax.ShapeDtypeStruct(tokens.shape, bf), jax.ShapeDtypeStruct(tokens.shape, bf),
+            jax.ShapeDtypeStruct((4, part, QKV_PAD), bf), jax.ShapeDtypeStruct((part, width), bf),
+            jax.ShapeDtypeStruct((4, part, 2 * fpart), bf), jax.ShapeDtypeStruct((fpart, width), bf),
+        ),
+        in_specs=[pl.BlockSpec(memory_space=pltpu.SMEM), vmem, vmem] + [any_space] * 7,
+        out_specs=[any_space] * 6,
+        scratch_shapes=list(scratch.values()),
+        compiler_params=pltpu.CompilerParams(
+            collective_id=1, has_side_effects=True, vmem_limit_bytes=VMEM_LIMIT),
+    )(length, cosine, sine, tokens, cotangent, packed, w_out, w_gate, w_up, w_down)
+    output, token_grad, grad_q, grad_out, grad_gu, grad_down = outs
+    pairs = grad_q[:, :, :6 * HEAD_DIM].reshape(4, part, 3, 2, HEAD_DIM).transpose(3, 1, 0, 2, 4).reshape(2, part, width)
+    values = grad_q[:, :, 6 * HEAD_DIM:9 * HEAD_DIM].transpose(1, 0, 2).reshape(part, width)
+    grad_qkv = jnp.concatenate([pairs[0], pairs[1], values], axis=1).astype(jnp.float32)
+    norms = jnp.sum(grad_q[:, :, 9 * HEAD_DIM:9 * HEAD_DIM + 4].astype(jnp.float32), axis=0)
+    halves = grad_gu.reshape(4, part, 2, fpart).transpose(2, 1, 0, 3).reshape(2, part, hidden).astype(jnp.float32)
+    return (
+        output, token_grad, grad_qkv[None], grad_out.astype(jnp.float32)[None], norms[:, 0][None], norms[:, 1][None],
+        halves[0][None], halves[1][None], grad_down.astype(jnp.float32)[None], norms[:, 2][None], norms[:, 3][None],
+    )
+
+
+def fits_relay(args):
+    tokens, lengths, w_qkv, w_gate, w_down = args[0], args[1], args[3], args[7], args[9]
+    axes = tuple(lax.axis_size(axis) for axis in ("section", "fsdp", "rep"))
+    return (
+        axes == (2, 4, 4)
+        and tokens.shape == (1, 1, BLOCK, 768)
+        and lengths.shape == (2, 1)
+        and w_qkv.shape == (1, 192, 2304)
+        and w_gate.shape == (1, 192, 3072)
+        and w_down.shape == (1, 768, 768)
+    )
+
+
+def program(*args):
+    return relay(*args) if fits_relay(args) else shards(*args)
+
+
 def solution(mesh):
     return jax.shard_map(
-        shards,
+        program,
         mesh=mesh,
         in_specs=(
             P("section", "rep", "fsdp", None),

time: 1240 us -> 355 us (0.29)
  waiting for transfers between devices: 781 us -> 0 us
  Pallas kernels: 0 us -> 309 us
  blocking collectives: 151 us -> 0 us
  matrix products: 146 us -> 0 us
  other arithmetic: 54.3 us -> 5.26 us
  local copies, waits for them, and re-layouts: 73.1 us -> 36 us
  between operations: 19.4 us -> 1.1 us
    reduce_scatter x5 -> x0, waiting for transfers between devices: 328 us -> none  [the longest x1 88 us: shards(): lax.psum_scatter(totals[6].astype(jnp.bfloat16), 'fsdp', scatter_dimensio...]
    pallas_call x0 -> x1, Pallas kernels: none -> 309 us  [relay(): pl.pallas_call(functools.partial(relay_kernel, tuple(scratch)), out_shape...]
    all_gather x5 -> x0, waiting for transfers between devices: 297 us -> none  [the longest x1 85 us: shards(): lax.all_gather(w_up[0], 'fsdp', axis=0, tiled=True)]
    dot_general x66 -> x0, matrix products: 146 us -> none  [the longest x3 17.2 us: layer_backward(): jnp.einsum('rd,re->de', inputs_low, grad_joined, preferred_element_type=j...]
    all_gather x6 -> x0, blocking collectives: 117 us -> none  [the longest x3 63.1 us: layer_forward(): lax.all_gather(value_own, 'fsdp', axis=0, tiled=True)]
    psum x1 -> x0, waiting for transfers between devices: 87.1 us -> none  [shards(): lax.psum(shares[0].astype(jnp.bfloat16), 'rep').astype(jnp.float32)]
    unnamed x23 -> x0, waiting for transfers between devices: 68.8 us -> none
    unnamed x477 -> x25, local copies, waits for them, and re-layouts: 40.1 us -> 5.5 us
  transfers between devices with their start and end apart: 23 -> 0, of which waited for: 14 -> 0; matrix products, arithmetic and copies ran while one was open for 13% -> 0% of each run, Pallas kernels for 0% -> 0%
where the time goes in v2:
time: 355 us; the launch traced here: 352 us
  Pallas kernels  309 us (87%)
  local copies, waits for them, and re-layouts  36 us (10%)
  other arithmetic  5.26 us (1%)
    pallas_call x1, Pallas kernels, relay(): pl.pallas_call(functools.partial(relay_kernel, tuple(scratch)), out_shape...  309 us
    slice x3, local copies, waits for them, and re-layouts, relay(): halves[1][None]  14.9 us

profile of v2, /device:TPU:0, one launch (start us, length us, event | category | flops | bytes accessed | tf_op | source)
XLA Modules:
  0.0 351.5 jit_solution(13873672898823316070)
XLA Ops:
  0.7 0.6 copy-done
  1.3 0.6 constant_dynamic-slice_fusion
  1.9 1.5 copy.43
  3.8 0.3 copy.47
  4.6 1.1 maximum_bitcast_fusion.wq_ref
  5.8 0.2 fusion.2
  6.1 0.8 copy.49.cos_ref
  6.9 0.8 copy.50.sin_ref
  7.8 309.2 %shard_map.203 = (bf16[1,1,128,768]{3,2,1,0:T(8,128)(2,1)}, bf16[1,1,128,768]{3,2,1,0:T(8,128)(2,1)}, bf16[4,192,640]{2,1,0:T(8,128)(2,1)}, bf16[192,768]{1,0:T(...) custom-call(s32[1]{0:T(128)} %bitcast.length_ref, f32[512,128]{1,0:T(8,128)} %copy.49.cos_ref, ...), custom_call_target="tpu_custom_call" | custom-call | tf_op jit(solution)/shard_map/pallas_call | solution.py:1126
  317.0 6.3 %reshape.197 = f32[4,192,2,768]{3,2,1,0:T(2,128)} reshape(bf16[4,192,1536]{2,1,0:T(8,128)(2,1)} %get-tuple-element.21) | data formatting | bytes 7077888 | tf_op jit(solution)/shard_map/convert_element_type | solution.py:1144
  323.2 9.4 %fusion.3 = (f32[1,192,4,768]{3,0,1,2:T(1,128)}, f32[1,192,4,768]{3,0,1,2:T(1,128)S(1)}) fusion(f32[2,192,4,768]{3,0,1,2:T(2,128)} %bitcast.33), kind=kLoop, calls=%fused_computation.21 | loop fusion | bytes 9437184 | tf_op jit(solution)/shard_map/slice | solution.py:1147
  332.6 1.5 copy.54
  334.2 2.3 slice.49
  336.4 3.2 copy.55
  339.6 2.3 slice.51
  341.9 0.3 copy.51
  342.3 1.0 slice_bitcast_fusion
  343.7 1.8 copy.56
  345.6 1.6 bitcast_convert_fusion
  347.1 0.9 bitcast_convert_fusion.1
  348.0 1.1 convert_reduce_fusion
  349.1 0.9 slice_reduce_fusion
  350.0 0.7 copy.64
  350.6 0.7 copy.65
  (37 shorter events, 1.4 us)
Async XLA Ops:
  0.6 0.7 copy-start
  3.5 0.8 copy-start.6
  3.5 0.8 copy-start.7
  3.5 0.8 copy-start.8
  3.5 0.8 copy-start.9
  339.6 2.3 copy-start.1
  343.7 1.8 copy-start.2
  345.5 1.6 copy-start.3
  345.6 4.4 %copy-start.5 = (bf16[1,1,128,768]{3,2,1,0:T(8,128)(2,1)S(1)}, bf16[1,1,128,768]{3,2,1,0:T(8,128)(2,1)}, u32[]{:S(2)}) copy-start(bf16[1,1,128,768]{3,2,1,0:T(8,128)(2,1)} %get-tuple-element.69) | copy-start | bytes 589828
  345.6 5.1 %copy-start.4 = (bf16[1,1,128,768]{3,2,1,0:T(8,128)(2,1)S(1)}, bf16[1,1,128,768]{3,2,1,0:T(8,128)(2,1)}, u32[]{:S(2)}) copy-start(bf16[1,1,128,768]{3,2,1,0:T(8,128)(2,1)} %get-tuple-element.70) | copy-start | bytes 589828

commit v3 on v2

--- a/solution.py
+++ b/solution.py
@@ -485,17 +485,20 @@
         s2o=vm((2, share, width), bf), s2d=vm((2, fshare, width), bf),
         r2q=vm((8, share, QKV_PAD), bf), r2g=vm((8, share, 2 * fpart), bf),
         r2o=vm((2, share, width), bf), r2d=vm((2, fshare, width), bf),
-        s3q=vm((4, share, QKV_PAD), bf), s3g=vm((4, share, 2 * fpart), bf),
+        s3q=vm((share, 3 * width + LANES), bf), s3g=vm((share, 2 * hidden), bf),
+        cos=vm((slots, LANES), f32), sin=vm((slots, LANES), f32), tab=dma((2,)),
         s3o=vm((share, width), bf), s3d=vm((fshare, width), bf),
         tok_s=dma((2,)), tok_r=dma, cot_s=dma((2,)), cot_r=dma, xc_s=dma((2,)), xc_r=dma((2,)),
-        wz=dma((2, 4, 4)), wss=dma((2, 2)), wso=dma((2, 2, 2)), wfs=dma((2, 4)), wp=dma((2, 4)),
+        wz=dma((2, 4, 4)), wss=dma((2, 2)), wso=dma((2, 2, 2)), wfs=dma((2, 4)), wrs=dma((2, 4)), wpx=dma((2, 4, 3)), wpy=dma((2, 4, 3)), wpd=dma((2, 4)),
         a_s=dma((2, 2)), a_r=dma((2, 2)), b_s=dma((2, 2)), b_r=dma((2, 2)), c_s=dma((8, 2)), c_r=dma((8, 2)),
-        s1s=dma((2, 4)), s1r=dma((2, 4)), s2s=dma((2, 4)), s2r=dma((4,)), s3s=dma((4,)), s3r=dma((4,)),
+        s1s=dma((2, 4)), s1a=dma((2, 4)), s1b=dma((2, 4)), s1t=dma((2, 4)), s1r=dma((2, 4)),
+        s2s=dma((2, 4)), s2r=dma((4,)),
+        s3s=dma((4, 2)), s3x=dma((4,)), s3y=dma((4,)), s3l=dma((4,)), s3t=dma((4,)), s3e=dma((4,)),
         o_s=dma((2,)), o_r=dma((2,)),
     )
 
 
-def relay_kernel(names, length_ref, cos_ref, sin_ref, tok_ref, cot_ref, wq_ref, wo_ref, wg_ref, wu_ref, wd_ref,
+def relay_kernel(names, length_ref, cos_in, sin_in, tok_ref, cot_ref, wq_ref, wo_ref, wg_ref, wu_ref, wd_ref,
                  out_ref, tg_ref, oq_ref, oo_ref, og_ref, od_ref, *scratch):
     m = types.SimpleNamespace(**dict(zip(names, scratch)))
     width = tok_ref.shape[3]
@@ -628,34 +631,55 @@
             source_own(l, O, "wait")
             source_own(l, D, "wait")
 
-    def pass_on(l, kind, here):
-        for k in (1, 2, 3):
-            block = weight[kind].at[l, here]
-            remote(block, block, m.wfs.at[l, kind], m.wp.at[l, kind], (s, z, r_of[k])).start()
-
-    def forward(l, kind):
+    xn, yn = (s, z, r_of[1]), (s, z, r_of[2])
+    cut = [3 * LANES, fpart, width // 2, width // 2]
+
+    def halves_of(kind, lanes):
+        return pl.ds(0, cut[kind]), pl.ds(cut[kind], lanes - cut[kind])
+
+    def block_rows(kind, k, rep):
         n = count[kind]
+        return rows((z_of[k] * part if kind in (Q, G) else 0) + rep * n, n)
+
+    def pass_on(l, kind, k):
+        block = weight[kind].at[l, block_rows(kind, k, r)]
+        wait_for(block, m.wz.at[l, kind, k if kind in (Q, G) else 0])
+        remote(block, block, m.wfs.at[l, kind], m.wpx.at[l, kind, k - 1], xn).start()
+        remote(block, block, m.wfs.at[l, kind], m.wpy.at[l, kind, k - 1], yn).start()
+
+    def pass_half(l, kind, k):
+        first, second = halves_of(kind, weight[kind].shape[2])
+        here = block_rows(kind, k, r_of[1])
+        wait_for(weight[kind].at[l, here], m.wpx.at[l, kind, k - 1])
+        half = weight[kind].at[l, here, first]
+        remote(half, half, m.wrs.at[l, kind], m.wpd.at[l, kind], yn).start()
+        here = block_rows(kind, k, r_of[2])
+        wait_for(weight[kind].at[l, here], m.wpy.at[l, kind, k - 1])
+        half = weight[kind].at[l, here, second]
+        remote(half, half, m.wrs.at[l, kind], m.wpd.at[l, kind], xn).start()
+
+    def each_block(kind, step):
         if kind in (Q, G):
             for k in (1, 2, 3):
-                here = rows(z_of[k] * part + r * n, n)
-                wait_for(weight[kind].at[l, here], m.wz.at[l, kind, k])
-                pass_on(l, kind, here)
+                step(k)
         else:
-            @pl.when(t != z)
-            def _():
-                here = rows(r * n, n)
-                wait_for(weight[kind].at[l, here], m.wz.at[l, kind, 0])
-                pass_on(l, kind, here)
+            pl.when(t != z)(lambda: step(1))
+
+    def forward(l, kind):
+        each_block(kind, lambda k: pass_on(l, kind, k))
+
+    def relay_on(l, kind):
+        each_block(kind, lambda k: pass_half(l, kind, k))
 
     def need(l, kind):
         n = count[kind]
         if kind in (Q, G):
             wait_for(weight[kind].at[l, rows(z * part, part)], m.wz.at[l, kind, 0])
-            wait_for(weight[kind].at[l, pl.ds(0, 9 * n)], m.wp.at[l, kind])
+            wait_for(weight[kind].at[l, pl.ds(0, 3 * n)], m.wpd.at[l, kind])
         else:
             @pl.when(t != z)
             def _():
-                wait_for(weight[kind].at[l, pl.ds(0, 3 * n)], m.wp.at[l, kind])
+                wait_for(weight[kind].at[l, pl.ds(0, n)], m.wpd.at[l, kind])
 
             @pl.when(t == z)
             def _():
@@ -663,12 +687,15 @@
 
     def forward_done(l, kind):
         n = count[kind]
+
+        def wait(blocks):
+            wait_for(weight[kind].at[l, pl.ds(0, 2 * blocks * n)], m.wfs.at[l, kind])
+            wait_for(weight[kind].at[l, pl.ds(0, blocks * n)], m.wrs.at[l, kind])
+
         if kind in (Q, G):
-            wait_for(weight[kind].at[l, pl.ds(0, 9 * n)], m.wfs.at[l, kind])
+            wait(3)
         else:
-            @pl.when(t != z)
-            def _():
-                wait_for(weight[kind].at[l, pl.ds(0, 3 * n)], m.wfs.at[l, kind])
+            pl.when(t != z)(lambda: wait(1))
 
     def own_rows(j):
         return rows((2 * j + s) * BLOCK, BLOCK)
@@ -708,7 +735,8 @@
 
     lane = lax.broadcasted_iota(jnp.int32, (BLOCK, LANES), 1)
     lane2 = lax.broadcasted_iota(jnp.int32, (BLOCK, 256), 1)
-    length = length_ref[0]
+    length = length_ref[zh, 0]
+    cos_ref, sin_ref = m.cos, m.sin
     live_keys = lax.broadcasted_iota(jnp.int32, (BLOCK, slots), 1) < length
     scale = HEAD_DIM ** (-0.5)
 
@@ -886,24 +914,46 @@
     third_out = [m.s3q, m.s3g, m.s3o, m.s3d]
     final = [oq_ref, og_ref, oo_ref, od_ref]
 
-    def spread_plane(l, kind):
+    def blocks_of(kind):
+        return range(4 if kind in (Q, G) else 1)
+
+    def grad_rows(kind, b, rep):
         n = count[kind]
-        for k in (1, 2, 3):
-            for b in range(4 if kind in (Q, G) else 1):
-                start = (b * part if kind in (Q, G) else 0) + r_of[k] * n
+        return rows((b * part if kind in (Q, G) else 0) + rep * n, n)
+
+    def plane_first(l, kind):
+        n = count[kind]
+        first, second = halves_of(kind, weight[kind].shape[2])
+        for b in blocks_of(kind):
+            for slot, rep in ((1, r_of[3]), (0, None)):
+                for lanes, device, near, sem in ((first, xn, r_of[1], m.s1a), (second, yn, r_of[2], m.s1b)):
+                    block = grad_rows(kind, b, near if rep is None else rep)
+                    remote(
+                        weight[kind].at[l, block, lanes], first_in[kind].at[l, slot, pl.ds(b * n, n), lanes],
+                        m.s1s.at[l, kind], sem.at[l, kind], device).start()
+
+    def plane_second(l, kind):
+        n = count[kind]
+        first, second = halves_of(kind, weight[kind].shape[2])
+        for lanes, device, rep, sem in ((first, yn, r_of[2], m.s1a), (second, xn, r_of[1], m.s1b)):
+            wait_for(first_in[kind].at[l, pl.ds(0, 2), :, lanes], sem.at[l, kind])
+            for b in blocks_of(kind):
+                block = grad_rows(kind, b, rep)
+                here = pl.ds(b * n, n)
+                weight[kind][l, block, lanes] = low(
+                    wide(weight[kind][l, block, lanes]) + wide(first_in[kind][l, 1, here, lanes]))
                 remote(
-                    weight[kind].at[l, rows(start, n)], first_in[kind].at[l, k - 1, pl.ds(b * n, n)],
-                    m.s1s.at[l, kind], m.s1r.at[l, kind], (s, z, r_of[k])).start()
+                    weight[kind].at[l, block, lanes], first_in[kind].at[l, 2, here, lanes],
+                    m.s1t.at[l, kind], m.s1r.at[l, kind], device).start()
 
     def spread_line(l, kind):
         n = count[kind]
-        wait_for(first_in[kind].at[l], m.s1r.at[l, kind])
-        for b in range(4 if kind in (Q, G) else 1):
-            start = (b * part if kind in (Q, G) else 0) + r * n
-            total = wide(weight[kind][l, rows(start, n)])
-            for k in range(3):
-                total += wide(first_in[kind][l, k, pl.ds(b * n, n)])
-            second_out[kind][l, pl.ds(b * n, n)] = low(total)
+        wait_for(first_in[kind].at[l, 2], m.s1r.at[l, kind])
+        for b in blocks_of(kind):
+            here = pl.ds(b * n, n)
+            total = wide(weight[kind][l, grad_rows(kind, b, r)])
+            total += wide(first_in[kind][l, 0, here]) + wide(first_in[kind][l, 2, here])
+            second_out[kind][l, here] = low(total)
         if kind in (Q, G):
             slot = 2 * z + s
             for k in range(4):
@@ -932,7 +982,8 @@
                 remote(src, dst, m.s2s.at[l, kind], m.s2r.at[kind], (l, t, r)).start()
 
     def line_done(l, kind):
-        wait_for(first_in[kind].at[l], m.s1s.at[l, kind])
+        wait_for(first_in[kind].at[l, pl.ds(0, 2)], m.s1s.at[l, kind])
+        wait_for(first_in[kind].at[l, 2], m.s1t.at[l, kind])
         n = count[kind]
         if kind in (Q, G):
             @pl.when(s == l)
@@ -947,25 +998,69 @@
             def _():
                 wait_for(second_out[kind].at[l], m.s2s.at[l, kind])
 
+    def in_order(parts):
+        low_half = lax.broadcasted_iota(jnp.int32, (share, LANES), 1) < HEAD_DIM
+
+        def swapped(values):
+            return pltpu.roll(values, HEAD_DIM, 1)
+
+        def pair(head):
+            return parts[head // 3][:, head % 3 * LANES:(head % 3 + 1) * LANES]
+
+        def value(head, at_low):
+            h = head % 3
+            start = 3 * LANES + h // 2 * LANES
+            values = parts[head // 3][:, start:start + LANES]
+            return values if (h != 1) == at_low else swapped(values)
+
+        for c in range(HEADS // 2):
+            even, odd = pair(2 * c), pair(2 * c + 1)
+            for i, values in enumerate((
+                jnp.where(low_half, even, swapped(odd)), jnp.where(low_half, swapped(even), odd),
+                jnp.where(low_half, value(2 * c, True), value(2 * c + 1, False)),
+            )):
+                m.s3q[:, pl.ds(i * width + c * LANES, LANES)] = low(values)
+        norms = sum(values[:, QKV_PAD - LANES:] for values in parts)
+        m.s3q[:, pl.ds(3 * width, LANES)] = low(norms)
+
+    def out_cut(kind):
+        lanes = third_out[kind].shape[1]
+        middle = lanes // 2 // LANES * LANES
+        return pl.ds(0, middle), pl.ds(middle, lanes - middle)
+
     def finish(kind):
-        n = count[kind]
         wait_for(second_in[kind], m.s2r.at[kind])
         if kind in (Q, G):
+            parts = []
             for b in range(4):
                 near = 2 * (b // 2) + b % 2
-                total = wide(second_in[kind][near]) + wide(second_in[kind][near + 4])
-                third_out[kind][b] = low(total)
-            dst = final[kind].at[:, rows(r * n, n), :]
+                parts.append(wide(second_in[kind][near]) + wide(second_in[kind][near + 4]))
+                if kind == G:
+                    for i in range(2):
+                        m.s3g[:, pl.ds((4 * i + b) * fpart, fpart)] = low(parts[b][:, i * fpart:(i + 1) * fpart])
+            if kind == Q:
+                in_order(parts)
         else:
             third_out[kind][...] = low(wide(second_in[kind][0]) + wide(second_in[kind][1]))
-            dst = final[kind].at[rows(r * n, n), :]
-        for k in (1, 2, 3):
-            remote(third_out[kind], dst, m.s3s.at[kind], m.s3r.at[kind], (s, z, r_of[k])).start()
-        pltpu.make_async_copy(third_out[kind], dst, m.s3r.at[kind]).start()
+        dst = final[kind].at[rows(r * count[kind], count[kind])]
+        remote(third_out[kind], dst, m.s3s.at[kind, 0], m.s3x.at[kind], xn).start()
+        remote(third_out[kind], dst, m.s3s.at[kind, 1], m.s3y.at[kind], yn).start()
+        pltpu.make_async_copy(third_out[kind], dst, m.s3l.at[kind]).start()
+
+    def finish_half(kind):
+        n = count[kind]
+        for lanes, rep, device, sem in zip(out_cut(kind), r_of[1:3], (yn, xn), (m.s3x, m.s3y)):
+            wait_for(final[kind].at[rows(rep * n, n)], sem.at[kind])
+            half = final[kind].at[rows(rep * n, n), lanes]
+            remote(half, half, m.s3t.at[kind], m.s3e.at[kind], device).start()
 
     def finish_done(kind):
-        wait_for(final[kind], m.s3r.at[kind])
-        wait_for(first_in[kind].at[0], m.s3s.at[kind])
+        block = final[kind].at[pl.ds(0, count[kind])]
+        wait_for(block, m.s3l.at[kind])
+        wait_for(block, m.s3e.at[kind])
+        wait_for(third_out[kind], m.s3s.at[kind, 0])
+        wait_for(third_out[kind], m.s3s.at[kind, 1])
+        wait_for(block, m.s3t.at[kind])
 
     def send_rows(i, src, dst, step):
         block = src.at[rows(zp * BLOCK, BLOCK)]
@@ -988,6 +1083,9 @@
             wait_for(dst, m.o_r.at[i])
 
     source(0)
+    tables = [pltpu.make_async_copy(src, dst, m.tab.at[i]) for i, (src, dst) in enumerate(((cos_in, m.cos), (sin_in, m.sin)))]
+    for copy in tables:
+        copy.start()
     scatter_rows(*cot_args, "start")
     for l in range(2):
         m.wo[l, pl.ds(part, 256 - part)] = jnp.zeros((256 - part, width), jnp.bfloat16)
@@ -1000,40 +1098,50 @@
         copy.start()
         halves.append(copy)
     forward(0, Q)
+    forward(0, O)
+    relay_on(0, Q)
+    relay_on(0, O)
+    for copy in tables:
+        copy.wait()
     need(0, Q)
     read_params(0)
     for j in range(2):
         halves[j].wait()
         project(0, j)
-    forward(0, O)
     forward(0, G)
     source(1)
     e = 0
     for l in range(2):
         attend(l)
         if l == 0:
+            relay_on(0, G)
             forward(0, D)
         need(l, O)
         a = [send_partial(e, j, m.mix.at[l], m.wo[l], dot) for j in range(2)]
         b = [send_sum(e, j, a[j]) for j in range(2)]
         if l == 0:
+            relay_on(0, D)
             forward(1, Q)
             forward(1, O)
+        else:
+            relay_on(1, D)
         c0 = finish_attention(e, l, 0, b[0])
         need(l, G)
-        need(l, D)
         c0.wait()
         feed(l, 0)
+        need(l, D)
         a0 = send_partial(e + 1, 0, m.act.at[l], m.wd[l], dot)
         c1 = finish_attention(e, l, 1, b[1])
         b0 = send_sum(e + 1, 0, a0)
+        if l == 0:
+            relay_on(1, Q)
+            relay_on(1, O)
         c1.wait()
         feed(l, 1)
         a1 = send_partial(e + 1, 1, m.act.at[l], m.wd[l], dot)
         b1 = send_sum(e + 1, 1, a1)
         if l == 0:
             forward(1, G)
-            forward(1, D)
             need(1, Q)
             read_params(1)
         e += 1
@@ -1042,6 +1150,9 @@
             if l == 0:
                 done.wait()
                 project(1, j)
+        if l == 0:
+            relay_on(1, G)
+            forward(1, D)
         e += 1
     send_rows(0, m.outb, out_ref.at[0, 0], "start")
     for l in range(2):
@@ -1061,10 +1172,14 @@
             a.append(send_partial(e, j, m.dgu, m.wgu[l], dot_rows))
         b0 = send_sum(e, 0, a[0])
         weight_grad(l, D)
-        spread_plane(l, D)
+        plane_first(l, D)
         b1 = send_sum(e, 1, a[1])
         weight_grad(l, G)
-        spread_plane(l, G)
+        plane_first(l, G)
+        if l == 0:
+            plane_second(1, O)
+            plane_second(1, Q)
+            spread_line(1, D)
         c = [back_first(e, l, j, copy) for j, copy in ((0, b0), (1, b1))]
         e += 1
         for j in range(2):
@@ -1074,26 +1189,47 @@
         a = [send_partial(e, j, m.dqkv, m.wq[l], dot_rows) for j in range(2)]
         b0 = send_sum(e, 0, a[0])
         weight_grad(l, O)
-        spread_plane(l, O)
+        plane_first(l, O)
         b1 = send_sum(e, 1, a[1])
         weight_grad(l, Q)
-        spread_plane(l, Q)
+        plane_first(l, Q)
+        plane_second(l, D)
         for j, copy in ((0, b0), (1, b1)):
             result = low(m.dres[kept(j)] + summed(e, j, copy))
             if l == 1:
                 m.dy[kept(j)] = wide(result)
             else:
                 m.tgb[kept(j)] = result
+        plane_second(l, G)
         e += 1
     send_rows(1, m.tgb, tg_ref.at[0, 0], "start")
-    for l in (1, 0):
+    for kind in (G, O, Q):
+        spread_line(1, kind)
+
+    @pl.when(s == 1)
+    def _():
         for kind in (D, G, O, Q):
-            spread_line(l, kind)
-
-        @pl.when(s == l)
-        def _():
-            for kind in (D, G, O, Q):
-                finish(kind)
+            finish(kind)
+    plane_second(0, O)
+    plane_second(0, Q)
+    for kind in (D, G, O, Q):
+        spread_line(0, kind)
+
+    @pl.when(s == 1)
+    def _():
+        for kind in (D, G, O, Q):
+            finish_half(kind)
+
+    @pl.when(s == 0)
+    def _():
+        finish(D)
+        finish(G)
+        finish_half(D)
+        finish(O)
+        finish_half(G)
+        finish(Q)
+        finish_half(O)
+        finish_half(Q)
     for kind in (D, G, O, Q):
         finish_done(kind)
         for l in (1, 0):
@@ -1113,7 +1249,6 @@
     sign = jnp.where(jnp.arange(HEAD_DIM) < HEAD_DIM // 2, -1.0, 1.0)
     cosine = jnp.tile(cosine[:, 0], (1, 2))
     sine = jnp.tile(sine[:, 0] * sign, (1, 2))
-    length = lax.dynamic_slice_in_dim(lengths[:, 0], lax.axis_index("fsdp") // 2, 1, 0)
     query, key, value = jnp.split(w_qkv[0], 3, axis=1)
     heads = (part, 4, 3, HEAD_DIM)
     joined = jnp.stack([query.reshape(heads), key.reshape(heads)], axis=3).reshape(part, 4, 6 * HEAD_DIM)
@@ -1121,30 +1256,27 @@
     norms = jnp.broadcast_to(jnp.pad(norms, ((0, 0), (0, HEAD_DIM - 4)))[:, None], (part, 4, HEAD_DIM))
     packed = jnp.concatenate([joined, value.reshape(part, 4, 3 * HEAD_DIM), norms], axis=2).transpose(1, 0, 2)
     scratch = relay_scratch(width, hidden)
-    any_space, vmem = pl.BlockSpec(memory_space=pl.ANY), pl.BlockSpec(memory_space=pltpu.VMEM)
+    any_space = pl.BlockSpec(memory_space=pl.ANY)
     fpart = hidden // 4
     outs = pl.pallas_call(
         functools.partial(relay_kernel, tuple(scratch)),
         out_shape=(
             jax.ShapeDtypeStruct(tokens.shape, bf), jax.ShapeDtypeStruct(tokens.shape, bf),
-            jax.ShapeDtypeStruct((4, part, QKV_PAD), bf), jax.ShapeDtypeStruct((part, width), bf),
-            jax.ShapeDtypeStruct((4, part, 2 * fpart), bf), jax.ShapeDtypeStruct((fpart, width), bf),
+            jax.ShapeDtypeStruct((part, 3 * width + LANES), bf), jax.ShapeDtypeStruct((part, width), bf),
+            jax.ShapeDtypeStruct((part, 2 * hidden), bf), jax.ShapeDtypeStruct((fpart, width), bf),
         ),
-        in_specs=[pl.BlockSpec(memory_space=pltpu.SMEM), vmem, vmem] + [any_space] * 7,
+        in_specs=[pl.BlockSpec(memory_space=pltpu.SMEM)] + [any_space] * 9,
         out_specs=[any_space] * 6,
         scratch_shapes=list(scratch.values()),
         compiler_params=pltpu.CompilerParams(
             collective_id=1, has_side_effects=True, vmem_limit_bytes=VMEM_LIMIT),
-    )(length, cosine, sine, tokens, cotangent, packed, w_out, w_gate, w_up, w_down)
+    )(lengths, cosine, sine, tokens, cotangent, packed, w_out, w_gate, w_up, w_down)
     output, token_grad, grad_q, grad_out, grad_gu, grad_down = outs
-    pairs = grad_q[:, :, :6 * HEAD_DIM].reshape(4, part, 3, 2, HEAD_DIM).transpose(3, 1, 0, 2, 4).reshape(2, part, width)
-    values = grad_q[:, :, 6 * HEAD_DIM:9 * HEAD_DIM].transpose(1, 0, 2).reshape(part, width)
-    grad_qkv = jnp.concatenate([pairs[0], pairs[1], values], axis=1).astype(jnp.float32)
-    norms = jnp.sum(grad_q[:, :, 9 * HEAD_DIM:9 * HEAD_DIM + 4].astype(jnp.float32), axis=0)
-    halves = grad_gu.reshape(4, part, 2, fpart).transpose(2, 1, 0, 3).reshape(2, part, hidden).astype(jnp.float32)
+    grad_q, grad_out, grad_gu, grad_down = (grad.astype(jnp.float32) for grad in (grad_q, grad_out, grad_gu, grad_down))
+    norms = grad_q[:, 3 * width + NORM_ROW:3 * width + NORM_ROW + 4]
     return (
-        output, token_grad, grad_qkv[None], grad_out.astype(jnp.float32)[None], norms[:, 0][None], norms[:, 1][None],
-        halves[0][None], halves[1][None], grad_down.astype(jnp.float32)[None], norms[:, 2][None], norms[:, 3][None],
+        output, token_grad, grad_q[None, :, :3 * width], grad_out[None], norms[:, 0][None], norms[:, 1][None],
+        grad_gu[None, :, :hidden], grad_gu[None, :, hidden:], grad_down[None], norms[:, 2][None], norms[:, 3][None],
     )
 
 

time: 355 us -> 309 us (0.87)
  local copies, waits for them, and re-layouts: 36 us -> 11.7 us
  Pallas kernels: 309 us -> 289 us
    pallas_call x1, Pallas kernels: 309 us -> 289 us  [relay(): pl.pallas_call(functools.partial(relay_kernel, tuple(scratch)), out_shape...]
    slice x8 -> x0, local copies, waits for them, and re-layouts: 19.1 us -> none  [the longest x3 14.9 us: relay(): halves[1][None]]
    convert_element_type x1 -> x0, local copies, waits for them, and re-layouts: 6.25 us -> none  [relay(): grad_gu.reshape(4, part, 2, fpart).transpose(2, 1, 0, 3)]
    broadcast_in_dim x0 -> x2, local copies, waits for them, and re-layouts: none -> 4.04 us  [the longest x1 2.72 us: relay(): grad_gu[None, :, hidden:]]
where the time goes in v3:
time: 309 us; the launch traced here: 308 us
  Pallas kernels  289 us (94%)
  local copies, waits for them, and re-layouts  11.7 us (4%)
  other arithmetic  6.02 us (2%)
    pallas_call x1, Pallas kernels, relay(): pl.pallas_call(functools.partial(relay_kernel, tuple(scratch)), out_shape...  289 us

profile of v3, /device:TPU:0, one launch (start us, length us, event | category | flops | bytes accessed | tf_op | source)
XLA Modules:
  0.0 308.0 jit_solution(16660835033237089272)
XLA Ops:
  0.6 1.5 copy.26
  2.2 0.1 fusion.3
  2.3 0.2 pad_maximum_fusion
  2.5 0.1 copy.27
  2.5 0.3 copy.30
  2.9 0.2 copy.31
  3.2 0.1 copy.37
  3.4 1.1 maximum_bitcast_fusion.wq_ref
  4.5 0.1 broadcast_multiply_fusion
  4.6 0.2 fusion.2
  4.9 0.8 copy.33.cos_in
  5.7 0.8 copy.34.sin_in
  6.6 0.6 copy.32.length_ref
  7.2 289.5 %shard_map.203 = (bf16[1,1,128,768]{3,2,1,0:T(8,128)(2,1)}, bf16[1,1,128,768]{3,2,1,0:T(8,128)(2,1)}, bf16[192,2432]{1,0:T(8,128)(2,1)}, bf16[192,768]{1,0:T(8,1...) custom-call(s32[2,1]{1,0:T(2,128)} %copy.32.length_ref, f32[512,128]{1,0:T(8,128)} %copy.33.cos_in, ...), custom_call_target="tpu_custom_call" | custom-call | tf_op jit(solution)/shard_map/pallas_call | solution.py:1261
  296.7 1.5 convert_element_type.20
  298.2 0.9 slice_reduce_fusion
  299.1 0.5 convert_element_type.21
  299.6 2.7 slice_bitcast_fusion
  302.4 1.3 slice_bitcast_fusion.2
  303.7 0.5 copy-done.1
  304.2 1.6 bitcast_convert_fusion
  305.8 0.9 bitcast_convert_fusion.1
  306.6 0.7 copy.40
  307.3 0.7 copy.41
  (27 shorter events, 0.2 us)
Async XLA Ops:
  2.4 0.7 copy-start.5
  2.4 0.7 copy-start.6
  2.4 0.7 copy-start.7
  2.5 0.7 copy-start.8
  3.4 3.2 %copy-start.9 = (s32[2,1]{0,1:T(1,128)S(1)}, s32[2,1]{0,1:T(1,128)}, u32[]{:S(2)}) copy-start(s32[2,1]{0,1:T(1,128)} %param.13) | copy-start | bytes 28
  296.7 2.4 copy-start
  302.4 1.8 copy-start.1
  303.7 2.1 copy-start.2
  304.2 2.4 copy-start.4
  304.2 3.1 %copy-start.3 = (bf16[1,1,128,768]{3,2,1,0:T(8,128)(2,1)S(1)}, bf16[1,1,128,768]{3,2,1,0:T(8,128)(2,1)}, u32[]{:S(2)}) copy-start(bf16[1,1,128,768]{3,2,1,0:T(8,128)(2,1)} %get-tuple-element.46) | copy-start | bytes 589828
